TPU v7x, 128 devices: a whole 4x4x4 slice. The times are simulated.
128 devices in a mesh: row: 8 (over x, y_hi), col: 16 (over y_lo, z, core).
Axes of the slice: x: 4, y: 4 (y_hi: 2, y_lo: 2; y = y_hi * 2 + y_lo), z: 4, core: 2. Of those that a mesh axis runs over, the one named last changes fastest.
Arguments:
- features: bfloat16 [65536, 256], P(('row', 'col')), may hold values from -4 to 4
- inject: bfloat16 [65536, 256], P(('row', 'col')), may hold values from -6 to 6
- weight: bfloat16 [256, 256], replicated, may hold values from -0.375 to 0.375
- tiles: bfloat16 [8, 16, 128, 256, 256], P('row', 'col'), may hold values from -0.046875 to 0.046875
- tile_rows: int32 [8, 16, 128], P('row', 'col'), may hold values from 0 to 31, as said below
- tile_cols: int32 [8, 16, 128], P('row', 'col'), may hold values from 0 to 15, as said below
- tile_count: int32 [8, 16], P('row', 'col'), may hold values from 32 to 128, as said below
- flags: int32 [256], P(('row', 'col')), may hold values 0 or 1
Outputs:
- states: bfloat16 [65536, 256], P(('row', 'col'))
- residual: float32 [256], P(('row', 'col'))
Inputs may be any that keep to these rules, and one draw needn't show every extreme that they name: `tile_count`: at most 128 live tiles at a grid position, exactly 128 at position (0, 0). `tile_rows`: no two tile slots of one grid position share both block row and block column. `tile_cols`: no two tile slots of one grid position share both block row and block column.
All inputs are finite; a program needn't handle non-finite values. No bound on the sum of `flags` on one device may be relied on, other than what follows from the above.
Results may differ from a plain program's by a relative error of at most 0.014.
Values may be sent and summed in bfloat16 or wider, within the bound.
No kernel may reach another device: no remote copies, remote signals or barrier semaphores. Data moves between devices by JAX's collectives and lax.ppermute only.
A program may use at most 128 MiB of HBM per device.

v0:
```python
import jax
import jax.numpy as jnp
from jax import lax
from jax.sharding import PartitionSpec as P

ITERS = 2


def per_device(features, inject, weight, tiles, tile_rows, tile_cols, tile_count, flags):
    tile_set = tiles[0, 0]
    rows_list = tile_rows[0, 0]
    cols_list = tile_cols[0, 0]
    count = tile_count[0, 0]
    block = tile_set.shape[-1]
    width = features.shape[1]
    own_rows = features.shape[0]
    n_col = lax.axis_size("col")
    keep = jnp.repeat(flags, block)[:, None] == 1
    state = features
    previous = features
    for step in range(ITERS):
        previous = state
        gathered = lax.all_gather(state, "row", axis=0, tiled=True)

        def add_tile(t, acc):
            source = lax.dynamic_slice_in_dim(gathered, cols_list[t] * block, block, 0)
            term = jnp.dot(tile_set[t], source, preferred_element_type=jnp.float32)
            where = rows_list[t] * block
            current = lax.dynamic_slice_in_dim(acc, where, block, 0)
            return lax.dynamic_update_slice_in_dim(acc, current + term, where, 0)

        partial_value = lax.fori_loop(
            0, count, add_tile, jnp.zeros((n_col * own_rows, width), jnp.float32)
        )
        totals = lax.psum(partial_value.astype(jnp.bfloat16), "col").astype(jnp.float32)
        summed = lax.dynamic_slice_in_dim(totals, lax.axis_index("col") * own_rows, own_rows, 0)
        aggregate = summed.astype(jnp.bfloat16)
        pre = jnp.dot(aggregate, weight, preferred_element_type=jnp.float32) + inject.astype(
            jnp.float32
        )
        update = jnp.tanh(pre).astype(jnp.bfloat16)
        state = jnp.where(keep, state, update)
    change = state.astype(jnp.float32) - previous.astype(jnp.float32)
    residual = jnp.sum((change * change).reshape(flags.shape[0], block * width), axis=1)
    return (state, residual)


def solution(mesh):
    in_specs = (
        P(("row", "col"), None),
        P(("row", "col"), None),
        P(),
        P("row", "col", None, None, None),
        P("row", "col", None),
        P("row", "col", None),
        P("row", "col"),
        P(("row", "col")),
    )
    out_specs = (P(("row", "col"), None), P(("row", "col")))
    return jax.shard_map(
        per_device, mesh=mesh, in_specs=in_specs, out_specs=out_specs, check_vma=False
    )
```

profile of v0, /device:TPU:6, one launch (start us, length us, event | category | flops | bytes accessed | tf_op | source)
XLA Modules:
  0.0 1726.9 jit_solution(4463316313475708881)
XLA Ops:
  8.0 59.4 %all-gather.3.cloned.1.call-done = bf16[4096,256]{1,0:T(8,128)(2,1)} async-done(((bf16[512,256]{1,0:T(8,128)(2,1)}), bf16[4096,256]{1,0:T(8,128)(2,1)}) %all-gather.3.cloned.1.call-update) | async-done | bytes 2097168 | tf_op jit(solution)/shard_map/all_gather | solution.py:23
  67.4 3.8 broadcast.12.clone
  71.1 371.0 %while.20 = (s32[]{:T(128)}, f32[8192,256]{1,0:T(8,128)}, s32[]{:T(128)}, s32[128]{0:T(128)S(1)}, bf16[128,256,256]{2,1,0:T(8,128)(2,1)}, /*index=5*/s32[128]{0:...) while((s32[]{:T(128)}, f32[8192,256]{1,0:T(8,128)}, ...), condition=%wide.region_1.0_spmd, body=%wide.region_0.0_spmd.sunk | while | flops 33619980 | bytes 786719 | solution.py:32
  442.2 5.8 convert_element_type.34
  448.5 412.9 %all-reduce.3.cloned.1.call-done = bf16[8192,256]{1,0:T(8,128)(2,1)} async-done(((bf16[8192,256]{1,0:T(8,128)(2,1)}), bf16[8192,256]{1,0:T(8,128)(2,1)}) %all-reduce.3.cloned.1.call-update) | async-done | bytes 4194320 | tf_op jit(solution)/shard_map/psum | solution.py:35
  863.4 58.6 %all-gather.5.cloned.1.call-done = bf16[4096,256]{0,1:T(8,128)(2,1)} async-done(((bf16[512,256]{0,1:T(8,128)(2,1)}), bf16[4096,256]{0,1:T(8,128)(2,1)}) %all-gather.5.cloned.1.call-update) | async-done | bytes 2097168 | tf_op jit(solution)/shard_map/all_gather | solution.py:23
  922.0 3.8 broadcast.12
  925.8 371.4 %while.21 = (s32[]{:T(128)}, f32[8192,256]{1,0:T(8,128)}, s32[]{:T(128)}, s32[128]{0:T(128)S(1)}, bf16[128,256,256]{2,1,0:T(8,128)(2,1)}, /*index=5*/s32[128]{0:...) while((s32[]{:T(128)}, f32[8192,256]{1,0:T(8,128)}, ...), condition=%wide.region_4.5_spmd, body=%wide.region_3.4_spmd.sunk | while | flops 33619980 | bytes 786719 | solution.py:32
  959.8 2.1 fusion.33
  965.0 2.0 fusion.33
  970.1 2.0 fusion.33
  1006.2 2.0 fusion.33
  1011.3 2.0 fusion.33
  1021.6 2.0 fusion.33
  1037.1 2.0 fusion.33
  1068.0 2.0 fusion.33
  1073.1 2.0 fusion.33
  1109.1 2.0 fusion.33
  1206.9 2.0 fusion.33
  1227.5 2.0 fusion.33
  1237.8 2.0 fusion.33
  1279.0 2.0 fusion.33
  1297.2 5.8 convert_element_type.39
  1303.0 414.6 %all-reduce.5.cloned.1.call-done = bf16[8192,256]{1,0:T(8,128)(2,1)} async-done(((bf16[8192,256]{1,0:T(8,128)(2,1)}), bf16[8192,256]{1,0:T(8,128)(2,1)}) %all-reduce.5.cloned.1.call-update) | async-done | bytes 4194320 | tf_op jit(solution)/shard_map/psum | solution.py:35
  (450 shorter events, 437.2 us)
Async XLA Ops:
  7.2 854.2 %copy-start = (bf16[256,256]{1,0:T(8,128)(2,1)S(1)}, bf16[256,256]{1,0:T(8,128)(2,1)}, u32[]{:S(2)}) copy-start(bf16[256,256]{1,0:T(8,128)(2,1)} %param.14) | copy-start | bytes 393220
  7.2 64.0 %copy-start.5 = (s32[1,1,128]{2,1,0:T(1,128)S(1)}, s32[1,1,128]{2,1,0:T(1,128)}, u32[]{:S(2)}) copy-start(s32[1,1,128]{2,1,0:T(1,128)} %param.16) | copy-start | bytes 1540
  7.2 63.9 %copy-start.6 = (s32[1,1,128]{2,1,0:T(1,128)S(1)}, s32[1,1,128]{2,1,0:T(1,128)}, u32[]{:S(2)}) copy-start(s32[1,1,128]{2,1,0:T(1,128)} %param.17) | copy-start | bytes 1540
  7.2 60.2 %all-gather.3.cloned.1.call-start = ((), (), s32[]{:S(2)}) async-start(), calls=%async_computation | async-start | bytes 2359296 | tf_op jit(solution)/shard_map/all_gather | solution.py:23
  7.9 853.5 %all-reduce.3.cloned.1.call-start = ((), (), s32[]{:S(2)}) async-start(), calls=%async_computation.1 | async-start | bytes 8388608 | tf_op jit(solution)/shard_map/psum | solution.py:35
  442.2 5.9 copy-start.1
  442.2 6.1 copy-start.3
  442.2 6.2 copy-start.4
  448.0 474.0 %all-gather.5.cloned.1.call-start = ((), (), s32[]{:S(2)}) async-start(), calls=%async_computation.2 | async-start | bytes 2359296 | tf_op jit(solution)/shard_map/all_gather | solution.py:23
  863.4 854.2 %all-reduce.5.cloned.1.call-start = ((), (), s32[]{:S(2)}) async-start(), calls=%async_computation.3 | async-start | bytes 8388608 | tf_op jit(solution)/shard_map/psum | solution.py:35
  1297.2 420.5 %copy-start.2 = (bf16[512,256]{0,1:T(8,128)(2,1)S(1)}, bf16[512,256]{0,1:T(8,128)(2,1)}, u32[]{:S(2)}) copy-start(bf16[512,256]{0,1:T(8,128)(2,1)} %fusion.15) | copy-start | bytes 786436
Sparse Core Ops, SparseCore 0:
  10.4 56.9 all-gather.2
  448.1 413.2 all-reduce.2
  864.2 57.7 all-gather.4
  1303.1 414.4 all-reduce.4
where the time goes:
time: 1740 us; the launch traced here: 1730 us
  waiting for transfers between devices  946 us (54%)
  matrix products  292 us (17%)
  loops' own time  283 us (16%)
  local copies, waits for them, and re-layouts  180 us (10%)
    psum x2, waiting for transfers between devices, per_device(): lax.psum(partial_value.astype(jnp.bfloat16), 'col').astype(jnp.float32)  828 us
    dot_general x144, matrix products, add_tile(): term = jnp.dot(tile_set[t], source, preferred_element_type=jnp.float32)  289 us
    another operation x2, loops' own time, per_device(): lax.fori_loop(0, count, add_tile, jnp.zeros((n_col * own_rows, width), jn...  283 us
    all_gather x2, waiting for transfers between devices, per_device(): gathered = lax.all_gather(state, 'row', axis=0, tiled=True)  118 us
    dynamic_slice x144, local copies, waits for them, and re-layouts, add_tile(): where = rows_list[t] * block  85.6 us
    dynamic_slice x144, local copies, waits for them, and re-layouts, add_tile(): source = lax.dynamic_slice_in_dim(gathered, cols_list[t] * block, block, 0)  85.3 us
  transfers between devices with their start and end apart: 4, of which 4 were waited for; matrix products, arithmetic and copies ran while one was open for 0% of the time, Pallas kernels for 0%

commit v1 on v0

v1 whole, which is shorter than its diff:
```python
import functools

import jax
import jax.numpy as jnp
from jax import lax
from jax.experimental import pallas as pl
from jax.experimental.pallas import tpu as pltpu
from jax.sharding import PartitionSpec as P

ITERS = 2
B = 256
BF = jnp.bfloat16
F32 = jnp.float32
N_SLOT = 32
UNROLL = 16
VMEM_LIMIT = 40 * 2**20


def col_perm(f):
    pairs = []
    for i in range(16):
        y, z, c = f(i // 8, i // 2 % 4, i % 2)
        pairs.append((i, (y % 2) * 8 + (z % 4) * 2 + c % 2))
    return pairs


def row_perm(f):
    pairs = []
    for i in range(8):
        x, y = f(i // 2, i % 2)
        pairs.append((i, (x % 4) * 2 + y % 2))
    return pairs


CORE = col_perm(lambda y, z, c: (y, z, c + 1))
Z_UP = col_perm(lambda y, z, c: (y, z + 1, c))
Z_DOWN = col_perm(lambda y, z, c: (y, z - 1, c))
Y_LO = col_perm(lambda y, z, c: (y + 1, z, c))
Y_HI = row_perm(lambda x, y: (x, y + 1))
X_UP = row_perm(lambda x, y: (x + 1, y))
X_DOWN = row_perm(lambda x, y: (x - 1, y))


def tile_words(rows, cols, count):
    row, col = lax.axis_index("row"), lax.axis_index("col")
    x, yh = row >> 1, row & 1
    yl, z, core = col >> 3, (col >> 1) & 3, col & 1
    half = ((rows >> 1) & 1) ^ core
    dst = (rows & 1) * 16 + half * 8 + (((rows >> 2) - z) & 3) * 2 + ((rows >> 4) ^ yl)
    src = (((cols >> 2) - x) & 3) * 4 + (((cols >> 1) & 1) ^ yh) * 2 + (cols & 1)
    live = jnp.arange(rows.shape[0], dtype=jnp.int32) < count
    return src + jnp.where(live, dst, N_SLOT) * 256


def tile_kernel(words, count, tiles, *refs):
    pieces, outs = refs[:16], refs[16:20]
    state, acc = refs[20:]
    acc[...] = jnp.zeros_like(acc)
    for s, piece in enumerate(pieces):
        state[s] = piece[...]

    @pl.loop(0, (count[0] + UNROLL - 1) // UNROLL)
    def _(i):
        for u in range(UNROLL):
            t = i * UNROLL + u
            word = words[t]
            acc[word >> 8] += jnp.dot(tiles[t], state[word & 255], preferred_element_type=F32)

    for i, out in enumerate(outs):
        for s in range(8):
            out[s] = acc[i * 8 + s].astype(BF)


def tile_sums(words, count, tiles, pieces):
    smem = pl.BlockSpec(memory_space=pltpu.SMEM)
    vmem = pl.BlockSpec(memory_space=pltpu.VMEM)
    out = jax.ShapeDtypeStruct((8, B, B), BF)
    return pl.pallas_call(
        tile_kernel,
        out_shape=(out,) * 4,
        in_specs=[smem, smem] + [vmem] * 17,
        out_specs=(vmem,) * 4,
        scratch_shapes=[
            pltpu.VMEM((16, B, B), BF),
            pltpu.VMEM((N_SLOT + 1, B, B), F32),
        ],
        compiler_params=pltpu.CompilerParams(vmem_limit_bytes=VMEM_LIMIT),
        cost_estimate=pl.CostEstimate(
            flops=128 * 2 * B**3, bytes_accessed=22 * 2**20, transcendentals=0
        ),
        name="tile_sums",
    )(words, count, tiles, *pieces)


def gather(block, chunk):
    near = lax.ppermute(block, "row", Y_HI)
    up = lax.ppermute(block, "row", X_UP)
    down = lax.ppermute(block, "row", X_DOWN)
    near_up = lax.ppermute(near, "row", X_UP)
    near_down = lax.ppermute(near, "row", X_DOWN)
    far = lax.ppermute(up, "row", X_UP)
    near_far = lax.ppermute(near_down, "row", X_DOWN)
    return [[block, near], [down, near_down], [far, near_far], [up, near_up]]


def add(*terms):
    total = terms[0].astype(F32)
    for term in terms[1:]:
        total = total + term.astype(F32)
    return total


def scatter_sum(keep, send):
    other = lax.ppermute(send, "col", CORE)
    far = add(keep[4:6], other[4:6]).astype(BF)
    from_low = lax.ppermute(far[0], "col", Z_UP)
    from_high = lax.ppermute(far[1], "col", Z_DOWN)
    up = jnp.stack([add(keep[2], other[2], from_low), add(keep[3], other[3])]).astype(BF)
    down = jnp.stack([add(keep[6], other[6]), add(keep[7], other[7], from_high)]).astype(BF)
    low = lax.ppermute(up, "col", Z_UP)
    high = lax.ppermute(down, "col", Z_DOWN)
    out = add(keep[1], other[1], low[1], high[1]).astype(BF)
    mine = add(keep[0], other[0], low[0], high[0])
    return mine, lax.ppermute(out, "col", Y_LO)


def per_device(features, inject, weight, tiles, tile_rows, tile_cols, tile_count, flags):
    count = tile_count[0]
    words = tile_words(tile_rows[0, 0], tile_cols[0, 0], count)
    tile_set = tiles[0, 0]
    blocks = [features[:B], features[B:]]
    previous = blocks
    for step in range(ITERS):
        previous = blocks
        parts = [gather(blocks[k], k) for k in range(2)]
        pieces = [parts[k][dx][dy] for dx in range(4) for dy in range(2) for k in range(2)]
        sums = tile_sums(words, count, tile_set, pieces)
        updated = []
        for k in range(2):
            mine, other = scatter_sum(sums[2 * k], sums[2 * k + 1])
            aggregate = add(mine, other).astype(BF)
            pre = jnp.dot(aggregate, weight, preferred_element_type=F32)
            pre = pre + inject[k * B : (k + 1) * B].astype(F32)
            updated.append(jnp.where(flags[k] == 1, blocks[k], jnp.tanh(pre).astype(BF)))
        blocks = updated
    change = [b.astype(F32) - p.astype(F32) for b, p in zip(blocks, previous)]
    residual = jnp.stack([jnp.sum(c * c) for c in change])
    return jnp.concatenate(blocks, axis=0), residual


def solution(mesh):
    in_specs = (
        P(("row", "col"), None),
        P(("row", "col"), None),
        P(),
        P("row", "col", None, None, None),
        P("row", "col", None),
        P("row", "col", None),
        P("row", "col"),
        P(("row", "col")),
    )
    out_specs = (P(("row", "col"), None), P(("row", "col")))
    return jax.shard_map(
        per_device, mesh=mesh, in_specs=in_specs, out_specs=out_specs, check_vma=False
    )
```

time: 1740 us -> 145 us (0.08)
  waiting for transfers between devices: 946 us -> 47.4 us
  matrix products: 292 us -> 2.21 us
  loops' own time: 283 us -> 0 us
  local copies, waits for them, and re-layouts: 180 us -> 1.79 us
  starting transfers between devices: 0.16 us -> 60.1 us
  Pallas kernels: 0 us -> 26 us
    psum x2 -> x0, waiting for transfers between devices: 828 us -> none  [per_device(): lax.psum(partial_value.astype(jnp.bfloat16), 'col').astype(jnp.float32)]
    dot_general x146 -> x4, matrix products: 292 us -> 2.21 us  [per_device(): pre = jnp.dot(aggregate, weight, preferred_element_type=F32)]
    another operation x2 -> x0, loops' own time: 283 us -> none  [per_device(): lax.fori_loop(0, count, add_tile, jnp.zeros((n_col * own_rows, width), jn...]
    dynamic_slice x288 -> x0, local copies, waits for them, and re-layouts: 171 us -> none  [the longest x144 85.6 us: add_tile(): where = rows_list[t] * block]
    all_gather x2 -> x0, waiting for transfers between devices: 118 us -> none  [per_device(): gathered = lax.all_gather(state, 'row', axis=0, tiled=True)]
    ppermute x0 -> x52, starting transfers between devices: none -> 60.1 us  [the longest x4 12.9 us: scatter_sum(): from_high = lax.ppermute(far[1], 'col', Z_DOWN)]
    ppermute x0 -> x52, waiting for transfers between devices: none -> 47.4 us  [the longest x4 13 us: scatter_sum(): low = lax.ppermute(up, 'col', Z_UP)]
    pallas_call x0 -> x2, Pallas kernels: none -> 26 us  [tile_sums(): pl.pallas_call(tile_kernel, out_shape=(out,) * 4, in_specs=[smem, smem] +...]
  transfers between devices with their start and end apart: 4 -> 52, of which waited for: 4 -> 24; matrix products, arithmetic and copies ran while one was open for 0% -> 3% of each run, Pallas kernels for 0% -> 0%
where the time goes in v1:
time: 145 us
  starting transfers between devices  60.1 us (41%)
  waiting for transfers between devices  47.4 us (33%)
  Pallas kernels  26 us (18%)
  other arithmetic  4.7 us (3%)
  between operations  2.99 us (2%)
  matrix products  2.21 us (2%)
  local copies, waits for them, and re-layouts  1.79 us (1%)
    pallas_call x2, Pallas kernels, tile_sums(): pl.pallas_call(tile_kernel, out_shape=(out,) * 4, in_specs=[smem, smem] +...  26 us
    ppermute x4, waiting for transfers between devices, scatter_sum(): low = lax.ppermute(up, 'col', Z_UP)  13 us
    ppermute x4, starting transfers between devices, scatter_sum(): from_high = lax.ppermute(far[1], 'col', Z_DOWN)  12.9 us
    ppermute x4, starting transfers between devices, scatter_sum(): high = lax.ppermute(down, 'col', Z_DOWN)  11.9 us
    ppermute x4, waiting for transfers between devices, gather(): near_far = lax.ppermute(near_down, 'row', X_DOWN)  8.78 us
    ppermute x4, starting transfers between devices, gather(): far = lax.ppermute(up, 'row', X_UP)  7.51 us
    ppermute x4, starting transfers between devices, gather(): near = lax.ppermute(block, 'row', Y_HI)  7.48 us
    ppermute x4, starting transfers between devices, gather(): near_up = lax.ppermute(near, 'row', X_UP)  6.33 us
  transfers between devices with their start and end apart: 52, of which 24 were waited for; matrix products, arithmetic and copies ran while one was open for 3% of the time, Pallas kernels for 0%

profile of v1, /device:TPU:6, one launch (start us, length us, event | category | flops | bytes accessed | tf_op | source)
XLA Modules:
  0.0 145.2 jit_solution(15734344850360594115)
XLA Ops:
  3.8 3.2 %collective-permute-start.1 = (bf16[256,256]{1,0:T(8,128)(2,1)S(1)}, bf16[256,256]{1,0:T(8,128)(2,1)S(1)}, u32[]{:S(2)}, u32[]{:S(2)}) collective-permute-start(bf16[256,256]{1,0:T(8,128)(2,1)S(1)} %get-tuple-element.42.refs_1_), channel_id=1, source_target_pairs={{0,16},{16,0},{32,48},{48,32},{64,80},{80,64},{96,112},{112,96},{1... | collective-permute-start | bytes 393224 | tf_op jit(solution)/shard_map/ppermute | solution.py:96
  9.4 2.8 %collective-permute-start.9 = (bf16[256,256]{1,0:T(8,128)(2,1)S(1)}, bf16[256,256]{1,0:T(8,128)(2,1)S(1)}, u32[]{:S(2)}, u32[]{:S(2)}) collective-permute-start(bf16[256,256]{1,0:T(8,128)(2,1)S(1)} %collective-permute-done.8.refs_13_), channel_id=1, source_target_pairs={{0,32},{16,48},{32,64},{48,80},{64,96},{80,112},{96,0},{112,16},{1... | collective-permute-start | bytes 393224 | tf_op jit(solution)/shard_map/ppermute | solution.py:101
  15.0 2.5 %collective-permute-start.13 = (bf16[256,256]{1,0:T(8,128)(2,1)S(1)}, bf16[256,256]{1,0:T(8,128)(2,1)S(1)}, u32[]{:S(2)}, u32[]{:S(2)}) collective-permute-start(bf16[256,256]{1,0:T(8,128)(2,1)S(1)} %collective-permute-done.1.refs_3_), channel_id=1, source_target_pairs={{0,32},{16,48},{32,64},{48,80},{64,96},{80,112},{96,0},{112,16},{1... | collective-permute-start | bytes 393224 | tf_op jit(solution)/shard_map/ppermute | solution.py:99
  22.2 2.3 %collective-permute-done.7.refs_8_ = bf16[256,256]{1,0:T(8,128)(2,1)S(1)} collective-permute-done((bf16[256,256]{1,0:T(8,128)(2,1)S(1)}, bf16[256,256]{1,0:T(8,128)(2,1)S(1)}, u32[]{:S(2)}, u32[]{:S(2)}) %collective-permute-start.7) | collective-permute-done | bytes 131104 | tf_op jit(solution)/shard_map/ppermute | solution.py:101
  27.4 13.0 %tile_sums.2 = (bf16[8,256,256]{2,1,0:T(8,128)(2,1)S(1)}, bf16[8,256,256]{2,1,0:T(8,128)(2,1)S(1)}, bf16[8,256,256]{2,1,0:T(8,128)(2,1)S(1)}, bf16[8,256,256]{2,1,0:T(8,128)(2,1)S(1)}) custom-call(s32[128]{0:T(128)S(1)} %fusion.57.words, s32[1]{0:T(128)} %bitcast.128.count, bf16[128,256,256]{2,1,0:T(8,128)(2,1)} %bitcast.130, ...), custom_call_target="tpu_custom_call" | custom-call | flops 4294967296 | bytes 23068672 | tf_op jit(solution)/shard_map/tile_sums/pallas_call | solution.py:78
  43.3 3.2 %collective-permute-start.17 = (bf16[256,256]{1,0:T(8,128)(2,1)S(1)}, bf16[256,256]{1,0:T(8,128)(2,1)S(1)}, u32[]{:S(2)}, u32[]{:S(2)}) collective-permute-start(bf16[256,256]{1,0:T(8,128)(2,1)S(1)} %get-tuple-element.39), channel_id=1, source_target_pairs={{0,6},{1,7},{2,0},{3,1},{4,2},{5,3},{6,4},{7,5},{8,14},{9,15},{10,... | collective-permute-start | bytes 393224 | tf_op jit(solution)/shard_map/ppermute | solution.py:117
  46.7 3.2 %collective-permute-start.23 = (bf16[256,256]{1,0:T(8,128)(2,1)S(1)}, bf16[256,256]{1,0:T(8,128)(2,1)S(1)}, u32[]{:S(2)}, u32[]{:S(2)}) collective-permute-start(bf16[256,256]{1,0:T(8,128)(2,1)S(1)} %get-tuple-element.41), channel_id=1, source_target_pairs={{0,6},{1,7},{2,0},{3,1},{4,2},{5,3},{6,4},{7,5},{8,14},{9,15},{10,... | collective-permute-start | bytes 393224 | tf_op jit(solution)/shard_map/ppermute | solution.py:117
  50.9 2.4 %collective-permute-start.18 = (bf16[2,256,256]{2,1,0:T(8,128)(2,1)S(1)}, bf16[2,256,256]{2,1,0:T(8,128)(2,1)S(1)}, u32[]{:S(2)}, u32[]{:S(2)}) collective-permute-start(bf16[2,256,256]{2,1,0:T(8,128)(2,1)S(1)} %pad_maximum_fusion.1), channel_id=1, source_target_pairs={{0,6},{1,7},{2,0},{3,1},{4,2},{5,3},{6,4},{7,5},{8,14},{9,15},{10,... | collective-permute-start | bytes 786440 | tf_op jit(solution)/shard_map/ppermute | solution.py:121
  53.5 3.3 %collective-permute-start.24 = (bf16[2,256,256]{2,1,0:T(8,128)(2,1)S(1)}, bf16[2,256,256]{2,1,0:T(8,128)(2,1)S(1)}, u32[]{:S(2)}, u32[]{:S(2)}) collective-permute-start(bf16[2,256,256]{2,1,0:T(8,128)(2,1)S(1)} %pad_maximum_fusion.3), channel_id=1, source_target_pairs={{0,6},{1,7},{2,0},{3,1},{4,2},{5,3},{6,4},{7,5},{8,14},{9,15},{10,... | collective-permute-start | bytes 786440 | tf_op jit(solution)/shard_map/ppermute | solution.py:121
  60.2 3.5 %collective-permute-done.16 = bf16[2,256,256]{2,1,0:T(8,128)(2,1)S(1)} collective-permute-done((bf16[2,256,256]{2,1,0:T(8,128)(2,1)S(1)}, bf16[2,256,256]{2,1,0:T(8,128)(2,1)S(1)}, u32[]{:S(2)}, u32[]{:S(2)}) %collective-permute-start.16) | collective-permute-done | bytes 262176 | tf_op jit(solution)/shard_map/ppermute | solution.py:120
  64.5 2.6 %collective-permute-done.22 = bf16[2,256,256]{2,1,0:T(8,128)(2,1)S(1)} collective-permute-done((bf16[2,256,256]{2,1,0:T(8,128)(2,1)S(1)}, bf16[2,256,256]{2,1,0:T(8,128)(2,1)S(1)}, u32[]{:S(2)}, u32[]{:S(2)}) %collective-permute-start.22) | collective-permute-done | bytes 262176 | tf_op jit(solution)/shard_map/ppermute | solution.py:120
  86.0 2.4 %collective-permute-start.35 = (bf16[256,256]{1,0:T(8,128)(2,1)S(1)}, bf16[256,256]{1,0:T(8,128)(2,1)S(1)}, u32[]{:S(2)}, u32[]{:S(2)}) collective-permute-start(bf16[256,256]{1,0:T(8,128)(2,1)S(1)} %collective-permute-done.34.refs_13_), channel_id=1, source_target_pairs={{0,32},{16,48},{32,64},{48,80},{64,96},{80,112},{96,0},{112,16},{1... | collective-permute-start | bytes 393224 | tf_op jit(solution)/shard_map/ppermute | solution.py:101
  88.4 2.4 %collective-permute-done.31.refs_7_ = bf16[256,256]{1,0:T(8,128)(2,1)S(1)} collective-permute-done((bf16[256,256]{1,0:T(8,128)(2,1)S(1)}, bf16[256,256]{1,0:T(8,128)(2,1)S(1)}, u32[]{:S(2)}, u32[]{:S(2)}) %collective-permute-start.31) | collective-permute-done | bytes 131104 | tf_op jit(solution)/shard_map/ppermute | solution.py:100
  91.0 3.6 %collective-permute-done.36.refs_10_ = bf16[256,256]{1,0:T(8,128)(2,1)S(1)} collective-permute-done((bf16[256,256]{1,0:T(8,128)(2,1)S(1)}, bf16[256,256]{1,0:T(8,128)(2,1)S(1)}, u32[]{:S(2)}, u32[]{:S(2)}) %collective-permute-start.36) | collective-permute-done | bytes 131104 | tf_op jit(solution)/shard_map/ppermute | solution.py:102
  94.6 2.4 %collective-permute-done.37.refs_11_ = bf16[256,256]{1,0:T(8,128)(2,1)S(1)} collective-permute-done((bf16[256,256]{1,0:T(8,128)(2,1)S(1)}, bf16[256,256]{1,0:T(8,128)(2,1)S(1)}, u32[]{:S(2)}, u32[]{:S(2)}) %collective-permute-start.37) | collective-permute-done | bytes 131104 | tf_op jit(solution)/shard_map/ppermute | solution.py:102
  97.0 13.0 %tile_sums.3 = (bf16[8,256,256]{2,1,0:T(8,128)(2,1)S(1)}, bf16[8,256,256]{2,1,0:T(8,128)(2,1)S(1)}, bf16[8,256,256]{2,1,0:T(8,128)(2,1)S(1)}, bf16[8,256,256]{2,1,0:T(8,128)(2,1)S(1)}) custom-call(s32[128]{0:T(128)S(1)} %fusion.57.words, s32[1]{0:T(128)} %bitcast.129.count, bf16[128,256,256]{2,1,0:T(8,128)(2,1)} %bitcast.131, ...), custom_call_target="tpu_custom_call" | custom-call | flops 4294967296 | bytes 23068672 | tf_op jit(solution)/shard_map/tile_sums/pallas_call | solution.py:78
  112.9 3.2 %collective-permute-start.43 = (bf16[256,256]{1,0:T(8,128)(2,1)S(1)}, bf16[256,256]{1,0:T(8,128)(2,1)S(1)}, u32[]{:S(2)}, u32[]{:S(2)}) collective-permute-start(bf16[256,256]{1,0:T(8,128)(2,1)S(1)} %get-tuple-element.35), channel_id=1, source_target_pairs={{0,6},{1,7},{2,0},{3,1},{4,2},{5,3},{6,4},{7,5},{8,14},{9,15},{10,... | collective-permute-start | bytes 393224 | tf_op jit(solution)/shard_map/ppermute | solution.py:117
  116.3 3.2 %collective-permute-start.49 = (bf16[256,256]{1,0:T(8,128)(2,1)S(1)}, bf16[256,256]{1,0:T(8,128)(2,1)S(1)}, u32[]{:S(2)}, u32[]{:S(2)}) collective-permute-start(bf16[256,256]{1,0:T(8,128)(2,1)S(1)} %get-tuple-element.37), channel_id=1, source_target_pairs={{0,6},{1,7},{2,0},{3,1},{4,2},{5,3},{6,4},{7,5},{8,14},{9,15},{10,... | collective-permute-start | bytes 393224 | tf_op jit(solution)/shard_map/ppermute | solution.py:117
  119.9 3.0 %collective-permute-start.44 = (bf16[2,256,256]{2,1,0:T(8,128)(2,1)S(1)}, bf16[2,256,256]{2,1,0:T(8,128)(2,1)S(1)}, u32[]{:S(2)}, u32[]{:S(2)}) collective-permute-start(bf16[2,256,256]{2,1,0:T(8,128)(2,1)S(1)} %pad_maximum_fusion.5), channel_id=1, source_target_pairs={{0,6},{1,7},{2,0},{3,1},{4,2},{5,3},{6,4},{7,5},{8,14},{9,15},{10,... | collective-permute-start | bytes 786440 | tf_op jit(solution)/shard_map/ppermute | solution.py:121
  123.1 3.3 %collective-permute-start.50 = (bf16[2,256,256]{2,1,0:T(8,128)(2,1)S(1)}, bf16[2,256,256]{2,1,0:T(8,128)(2,1)S(1)}, u32[]{:S(2)}, u32[]{:S(2)}) collective-permute-start(bf16[2,256,256]{2,1,0:T(8,128)(2,1)S(1)} %pad_maximum_fusion.7), channel_id=1, source_target_pairs={{0,6},{1,7},{2,0},{3,1},{4,2},{5,3},{6,4},{7,5},{8,14},{9,15},{10,... | collective-permute-start | bytes 786440 | tf_op jit(solution)/shard_map/ppermute | solution.py:121
  126.5 3.1 %collective-permute-done.44 = bf16[2,256,256]{2,1,0:T(8,128)(2,1)S(1)} collective-permute-done((bf16[2,256,256]{2,1,0:T(8,128)(2,1)S(1)}, bf16[2,256,256]{2,1,0:T(8,128)(2,1)S(1)}, u32[]{:S(2)}, u32[]{:S(2)}) %collective-permute-start.44) | collective-permute-done | bytes 262176 | tf_op jit(solution)/shard_map/ppermute | solution.py:121
  129.6 3.8 %collective-permute-done.42 = bf16[2,256,256]{2,1,0:T(8,128)(2,1)S(1)} collective-permute-done((bf16[2,256,256]{2,1,0:T(8,128)(2,1)S(1)}, bf16[2,256,256]{2,1,0:T(8,128)(2,1)S(1)}, u32[]{:S(2)}, u32[]{:S(2)}) %collective-permute-start.42) | collective-permute-done | bytes 262176 | tf_op jit(solution)/shard_map/ppermute | solution.py:120
  133.5 3.1 %collective-permute-done.48 = bf16[2,256,256]{2,1,0:T(8,128)(2,1)S(1)} collective-permute-done((bf16[2,256,256]{2,1,0:T(8,128)(2,1)S(1)}, bf16[2,256,256]{2,1,0:T(8,128)(2,1)S(1)}, u32[]{:S(2)}, u32[]{:S(2)}) %collective-permute-start.48) | collective-permute-done | bytes 262176 | tf_op jit(solution)/shard_map/ppermute | solution.py:120
  136.8 3.0 %collective-permute-done.45 = bf16[256,256]{1,0:T(8,128)(2,1)S(1)} collective-permute-done((bf16[256,256]{1,0:T(8,128)(2,1)S(1)}, bf16[256,256]{1,0:T(8,128)(2,1)S(1)}, u32[]{:S(2)}, u32[]{:S(2)}) %collective-permute-start.45) | collective-permute-done | bytes 131104 | tf_op jit(solution)/shard_map/ppermute | solution.py:124
  (127 shorter events, 50.8 us)
Async XLA Ops:
  1.7 7.2 %collective-permute-start.8 = (bf16[256,256]{1,0:T(8,128)(2,1)S(1)}, bf16[256,256]{1,0:T(8,128)(2,1)S(1)}, u32[]{:S(2)}, u32[]{:S(2)}) collective-permute-start(bf16[256,256]{1,0:T(8,128)(2,1)S(1)} %get-tuple-element.42.refs_1_), channel_id=1, source_target_pairs={{0,32},{16,48},{32,64},{48,80},{64,96},{80,112},{96,0},{112,16},{1... | collective-permute-start | bytes 393224 | tf_op jit(solution)/shard_map/ppermute | solution.py:97
  3.8 8.4 %collective-permute-start.1 = (bf16[256,256]{1,0:T(8,128)(2,1)S(1)}, bf16[256,256]{1,0:T(8,128)(2,1)S(1)}, u32[]{:S(2)}, u32[]{:S(2)}) collective-permute-start(bf16[256,256]{1,0:T(8,128)(2,1)S(1)} %get-tuple-element.42.refs_1_), channel_id=1, source_target_pairs={{0,16},{16,0},{32,48},{48,32},{64,80},{80,64},{96,112},{112,96},{1... | collective-permute-start | bytes 393224 | tf_op jit(solution)/shard_map/ppermute | solution.py:96
  7.4 7.6 %collective-permute-start.6 = (bf16[256,256]{1,0:T(8,128)(2,1)S(1)}, bf16[256,256]{1,0:T(8,128)(2,1)S(1)}, u32[]{:S(2)}, u32[]{:S(2)}) collective-permute-start(bf16[256,256]{1,0:T(8,128)(2,1)S(1)} %get-tuple-element.43.refs_0_), channel_id=1, source_target_pairs={{0,32},{16,48},{32,64},{48,80},{64,96},{80,112},{96,0},{112,16},{1... | collective-permute-start | bytes 393224 | tf_op jit(solution)/shard_map/ppermute | solution.py:97
  9.0 8.5 %collective-permute-start.2 = (bf16[256,256]{1,0:T(8,128)(2,1)S(1)}, bf16[256,256]{1,0:T(8,128)(2,1)S(1)}, u32[]{:S(2)}, u32[]{:S(2)}) collective-permute-start(bf16[256,256]{1,0:T(8,128)(2,1)S(1)} %get-tuple-element.43.refs_0_), channel_id=1, source_target_pairs={{0,96},{16,112},{32,0},{48,16},{64,32},{80,48},{96,64},{112,80},{1... | collective-permute-start | bytes 393224 | tf_op jit(solution)/shard_map/ppermute | solution.py:98
  9.4 8.8 %collective-permute-start.9 = (bf16[256,256]{1,0:T(8,128)(2,1)S(1)}, bf16[256,256]{1,0:T(8,128)(2,1)S(1)}, u32[]{:S(2)}, u32[]{:S(2)}) collective-permute-start(bf16[256,256]{1,0:T(8,128)(2,1)S(1)} %collective-permute-done.8.refs_13_), channel_id=1, source_target_pairs={{0,32},{16,48},{32,64},{48,80},{64,96},{80,112},{96,0},{112,16},{1... | collective-permute-start | bytes 393224 | tf_op jit(solution)/shard_map/ppermute | solution.py:101
  13.5 7.7 %collective-permute-start.4 = (bf16[256,256]{1,0:T(8,128)(2,1)S(1)}, bf16[256,256]{1,0:T(8,128)(2,1)S(1)}, u32[]{:S(2)}, u32[]{:S(2)}) collective-permute-start(bf16[256,256]{1,0:T(8,128)(2,1)S(1)} %collective-permute-done.refs_2_), channel_id=1, source_target_pairs={{0,96},{16,112},{32,0},{48,16},{64,32},{80,48},{96,64},{112,80},{1... | collective-permute-start | bytes 393224 | tf_op jit(solution)/shard_map/ppermute | solution.py:100
  15.0 7.2 %collective-permute-start.13 = (bf16[256,256]{1,0:T(8,128)(2,1)S(1)}, bf16[256,256]{1,0:T(8,128)(2,1)S(1)}, u32[]{:S(2)}, u32[]{:S(2)}) collective-permute-start(bf16[256,256]{1,0:T(8,128)(2,1)S(1)} %collective-permute-done.1.refs_3_), channel_id=1, source_target_pairs={{0,32},{16,48},{32,64},{48,80},{64,96},{80,112},{96,0},{112,16},{1... | collective-permute-start | bytes 393224 | tf_op jit(solution)/shard_map/ppermute | solution.py:99
  43.3 7.4 %collective-permute-start.17 = (bf16[256,256]{1,0:T(8,128)(2,1)S(1)}, bf16[256,256]{1,0:T(8,128)(2,1)S(1)}, u32[]{:S(2)}, u32[]{:S(2)}) collective-permute-start(bf16[256,256]{1,0:T(8,128)(2,1)S(1)} %get-tuple-element.39), channel_id=1, source_target_pairs={{0,6},{1,7},{2,0},{3,1},{4,2},{5,3},{6,4},{7,5},{8,14},{9,15},{10,... | collective-permute-start | bytes 393224 | tf_op jit(solution)/shard_map/ppermute | solution.py:117
  50.9 9.4 %collective-permute-start.18 = (bf16[2,256,256]{2,1,0:T(8,128)(2,1)S(1)}, bf16[2,256,256]{2,1,0:T(8,128)(2,1)S(1)}, u32[]{:S(2)}, u32[]{:S(2)}) collective-permute-start(bf16[2,256,256]{2,1,0:T(8,128)(2,1)S(1)} %pad_maximum_fusion.1), channel_id=1, source_target_pairs={{0,6},{1,7},{2,0},{3,1},{4,2},{5,3},{6,4},{7,5},{8,14},{9,15},{10,... | collective-permute-start | bytes 786440 | tf_op jit(solution)/shard_map/ppermute | solution.py:121
  53.2 10.5 %collective-permute-start.16 = (bf16[2,256,256]{2,1,0:T(8,128)(2,1)S(1)}, bf16[2,256,256]{2,1,0:T(8,128)(2,1)S(1)}, u32[]{:S(2)}, u32[]{:S(2)}) collective-permute-start(bf16[2,256,256]{2,1,0:T(8,128)(2,1)S(1)} %pad_maximum_fusion), channel_id=1, source_target_pairs={{0,2},{1,3},{2,4},{3,5},{4,6},{5,7},{6,0},{7,1},{8,10},{9,11},{10,... | collective-permute-start | bytes 786440 | tf_op jit(solution)/shard_map/ppermute | solution.py:120
  53.5 11.0 %collective-permute-start.24 = (bf16[2,256,256]{2,1,0:T(8,128)(2,1)S(1)}, bf16[2,256,256]{2,1,0:T(8,128)(2,1)S(1)}, u32[]{:S(2)}, u32[]{:S(2)}) collective-permute-start(bf16[2,256,256]{2,1,0:T(8,128)(2,1)S(1)} %pad_maximum_fusion.3), channel_id=1, source_target_pairs={{0,6},{1,7},{2,0},{3,1},{4,2},{5,3},{6,4},{7,5},{8,14},{9,15},{10,... | collective-permute-start | bytes 786440 | tf_op jit(solution)/shard_map/ppermute | solution.py:121
  56.8 10.3 %collective-permute-start.22 = (bf16[2,256,256]{2,1,0:T(8,128)(2,1)S(1)}, bf16[2,256,256]{2,1,0:T(8,128)(2,1)S(1)}, u32[]{:S(2)}, u32[]{:S(2)}) collective-permute-start(bf16[2,256,256]{2,1,0:T(8,128)(2,1)S(1)} %pad_maximum_fusion.2), channel_id=1, source_target_pairs={{0,2},{1,3},{2,4},{3,5},{4,6},{5,7},{6,0},{7,1},{8,10},{9,11},{10,... | collective-permute-start | bytes 786440 | tf_op jit(solution)/shard_map/ppermute | solution.py:120
  67.1 7.4 %collective-permute-start.25 = (bf16[256,256]{1,0:T(8,128)(2,1)S(1)}, bf16[256,256]{1,0:T(8,128)(2,1)S(1)}, u32[]{:S(2)}, u32[]{:S(2)}) collective-permute-start(bf16[256,256]{1,0:T(8,128)(2,1)S(1)} %fusion.25), channel_id=1, source_target_pairs={{0,8},{1,9},{2,10},{3,11},{4,12},{5,13},{6,14},{7,15},{8,0},{9,1},... | collective-permute-start | bytes 393224 | tf_op jit(solution)/shard_map/ppermute | solution.py:124
  70.3 7.2 %collective-permute-start.32 = (bf16[256,256]{1,0:T(8,128)(2,1)S(1)}, bf16[256,256]{1,0:T(8,128)(2,1)S(1)}, u32[]{:S(2)}, u32[]{:S(2)}) collective-permute-start(bf16[256,256]{1,0:T(8,128)(2,1)S(1)} %fusion.11.refs_0_), channel_id=1, source_target_pairs={{0,32},{16,48},{32,64},{48,80},{64,96},{80,112},{96,0},{112,16},{1... | collective-permute-start | bytes 393224 | tf_op jit(solution)/shard_map/ppermute | solution.py:97
  70.4 8.2 %collective-permute-start.28 = (bf16[256,256]{1,0:T(8,128)(2,1)S(1)}, bf16[256,256]{1,0:T(8,128)(2,1)S(1)}, u32[]{:S(2)}, u32[]{:S(2)}) collective-permute-start(bf16[256,256]{1,0:T(8,128)(2,1)S(1)} %fusion.11.refs_0_), channel_id=1, source_target_pairs={{0,96},{16,112},{32,0},{48,16},{64,32},{80,48},{96,64},{112,80},{1... | collective-permute-start | bytes 393224 | tf_op jit(solution)/shard_map/ppermute | solution.py:98
  72.4 8.4 %collective-permute-start.26 = (bf16[256,256]{1,0:T(8,128)(2,1)S(1)}, bf16[256,256]{1,0:T(8,128)(2,1)S(1)}, u32[]{:S(2)}, u32[]{:S(2)}) collective-permute-start(bf16[256,256]{1,0:T(8,128)(2,1)S(1)} %fusion.11.refs_0_), channel_id=1, source_target_pairs={{0,16},{16,0},{32,48},{48,32},{64,80},{80,64},{96,112},{112,96},{1... | collective-permute-start | bytes 393224 | tf_op jit(solution)/shard_map/ppermute | solution.py:96
  78.6 7.4 %collective-permute-start.33 = (bf16[256,256]{1,0:T(8,128)(2,1)S(1)}, bf16[256,256]{1,0:T(8,128)(2,1)S(1)}, u32[]{:S(2)}, u32[]{:S(2)}) collective-permute-start(bf16[256,256]{1,0:T(8,128)(2,1)S(1)} %collective-permute-done.32.refs_12_), channel_id=1, source_target_pairs={{0,32},{16,48},{32,64},{48,80},{64,96},{80,112},{96,0},{112,16},{1... | collective-permute-start | bytes 393224 | tf_op jit(solution)/shard_map/ppermute | solution.py:101
  80.8 7.6 %collective-permute-start.30 = (bf16[256,256]{1,0:T(8,128)(2,1)S(1)}, bf16[256,256]{1,0:T(8,128)(2,1)S(1)}, u32[]{:S(2)}, u32[]{:S(2)}) collective-permute-start(bf16[256,256]{1,0:T(8,128)(2,1)S(1)} %collective-permute-done.26.refs_2_), channel_id=1, source_target_pairs={{0,96},{16,112},{32,0},{48,16},{64,32},{80,48},{96,64},{112,80},{1... | collective-permute-start | bytes 393224 | tf_op jit(solution)/shard_map/ppermute | solution.py:100
  81.4 9.4 %collective-permute-start.31 = (bf16[256,256]{1,0:T(8,128)(2,1)S(1)}, bf16[256,256]{1,0:T(8,128)(2,1)S(1)}, u32[]{:S(2)}, u32[]{:S(2)}) collective-permute-start(bf16[256,256]{1,0:T(8,128)(2,1)S(1)} %collective-permute-done.27.refs_3_), channel_id=1, source_target_pairs={{0,96},{16,112},{32,0},{48,16},{64,32},{80,48},{96,64},{112,80},{1... | collective-permute-start | bytes 393224 | tf_op jit(solution)/shard_map/ppermute | solution.py:100
  82.9 7.9 %collective-permute-start.38 = (bf16[256,256]{1,0:T(8,128)(2,1)S(1)}, bf16[256,256]{1,0:T(8,128)(2,1)S(1)}, u32[]{:S(2)}, u32[]{:S(2)}) collective-permute-start(bf16[256,256]{1,0:T(8,128)(2,1)S(1)} %collective-permute-done.26.refs_2_), channel_id=1, source_target_pairs={{0,32},{16,48},{32,64},{48,80},{64,96},{80,112},{96,0},{112,16},{1... | collective-permute-start | bytes 393224 | tf_op jit(solution)/shard_map/ppermute | solution.py:99
  119.9 9.7 %collective-permute-start.44 = (bf16[2,256,256]{2,1,0:T(8,128)(2,1)S(1)}, bf16[2,256,256]{2,1,0:T(8,128)(2,1)S(1)}, u32[]{:S(2)}, u32[]{:S(2)}) collective-permute-start(bf16[2,256,256]{2,1,0:T(8,128)(2,1)S(1)} %pad_maximum_fusion.5), channel_id=1, source_target_pairs={{0,6},{1,7},{2,0},{3,1},{4,2},{5,3},{6,4},{7,5},{8,14},{9,15},{10,... | collective-permute-start | bytes 786440 | tf_op jit(solution)/shard_map/ppermute | solution.py:121
  122.8 10.5 %collective-permute-start.42 = (bf16[2,256,256]{2,1,0:T(8,128)(2,1)S(1)}, bf16[2,256,256]{2,1,0:T(8,128)(2,1)S(1)}, u32[]{:S(2)}, u32[]{:S(2)}) collective-permute-start(bf16[2,256,256]{2,1,0:T(8,128)(2,1)S(1)} %pad_maximum_fusion.4), channel_id=1, source_target_pairs={{0,2},{1,3},{2,4},{3,5},{4,6},{5,7},{6,0},{7,1},{8,10},{9,11},{10,... | collective-permute-start | bytes 786440 | tf_op jit(solution)/shard_map/ppermute | solution.py:120
  123.1 10.4 %collective-permute-start.50 = (bf16[2,256,256]{2,1,0:T(8,128)(2,1)S(1)}, bf16[2,256,256]{2,1,0:T(8,128)(2,1)S(1)}, u32[]{:S(2)}, u32[]{:S(2)}) collective-permute-start(bf16[2,256,256]{2,1,0:T(8,128)(2,1)S(1)} %pad_maximum_fusion.7), channel_id=1, source_target_pairs={{0,6},{1,7},{2,0},{3,1},{4,2},{5,3},{6,4},{7,5},{8,14},{9,15},{10,... | collective-permute-start | bytes 786440 | tf_op jit(solution)/shard_map/ppermute | solution.py:121
  126.4 10.3 %collective-permute-start.48 = (bf16[2,256,256]{2,1,0:T(8,128)(2,1)S(1)}, bf16[2,256,256]{2,1,0:T(8,128)(2,1)S(1)}, u32[]{:S(2)}, u32[]{:S(2)}) collective-permute-start(bf16[2,256,256]{2,1,0:T(8,128)(2,1)S(1)} %pad_maximum_fusion.6), channel_id=1, source_target_pairs={{0,2},{1,3},{2,4},{3,5},{4,6},{5,7},{6,0},{7,1},{8,10},{9,11},{10,... | collective-permute-start | bytes 786440 | tf_op jit(solution)/shard_map/ppermute | solution.py:120
  (32 other events, 437.0 us)

commit v2 on v1

v2 whole, which is shorter than its diff:
```python
import functools

import jax
import jax.numpy as jnp
from jax import lax
from jax.experimental import pallas as pl
from jax.experimental.pallas import tpu as pltpu
from jax.sharding import PartitionSpec as P

ITERS = 2
B = 256
BF = jnp.bfloat16
F32 = jnp.float32
N_SLOT = 32
N_EARLY = 10
GROUP = 16
VMEM_LIMIT = 16 * 2**20
PIECES = 0x53726410


def col_perm(f):
    pairs = []
    for i in range(16):
        y, z, c = f(i // 8, i // 2 % 4, i % 2)
        pairs.append((i, (y % 2) * 8 + (z % 4) * 2 + c % 2))
    return pairs


def row_perm(f):
    pairs = []
    for i in range(8):
        x, y = f(i // 2, i % 2)
        pairs.append((i, (x % 4) * 2 + y % 2))
    return pairs


CORE = col_perm(lambda y, z, c: (y, z, c + 1))
Z_UP = col_perm(lambda y, z, c: (y, z + 1, c))
Z_DOWN = col_perm(lambda y, z, c: (y, z - 1, c))
Y_LO = col_perm(lambda y, z, c: (y + 1, z, c))
Y_HI = row_perm(lambda x, y: (x, y + 1))
X_UP = row_perm(lambda x, y: (x + 1, y))
X_DOWN = row_perm(lambda x, y: (x - 1, y))
X_FAR = row_perm(lambda x, y: (x + 2, y))


SMEM = pl.BlockSpec(memory_space=pltpu.SMEM)
VMEM = pl.BlockSpec(memory_space=pltpu.VMEM)
HBM = pl.BlockSpec(memory_space=pltpu.HBM)
PARAMS = pltpu.CompilerParams(vmem_limit_bytes=VMEM_LIMIT)


def cost(n_tiles, extra):
    return pl.CostEstimate(
        flops=n_tiles * 2 * B**3, bytes_accessed=extra, transcendentals=0
    )


def tile_words(rows, cols, count):
    row, col = lax.axis_index("row"), lax.axis_index("col")
    x, yh = row >> 1, row & 1
    yl, z, core = col >> 3, (col >> 1) & 3, col & 1
    half = ((rows >> 1) & 1) ^ core
    dst = (rows & 1) * 16 + half * 8 + (((rows >> 2) - z) & 3) * 2 + ((rows >> 4) ^ yl)
    place = (((cols >> 2) - x) & 3) * 2 + (((cols >> 1) & 1) ^ yh)
    src = ((PIECES >> (place * 4)) & 15) * 2 + (cols & 1)
    index = jnp.arange(rows.shape[0], dtype=jnp.int32)
    live = index < count
    early = live & (src < N_EARLY)
    word = index + src * 256 + dst * 65536
    key = jnp.where(early, 0, jnp.where(live, 1, 2)) * 256 + index
    rank = jnp.sum((key[None, :] < key[:, None]).astype(jnp.int32), axis=1)
    words = jnp.sum(jnp.where(rank[:, None] == index[None, :], word[:, None], 0), axis=0)
    return words, jnp.stack([jnp.sum(early.astype(jnp.int32)), count[0]])


def copy_kernel(source, target, sem):
    copy = pltpu.make_async_copy(source, target, sem)
    copy.start()
    copy.wait()


def copy_in(value):
    return pl.pallas_call(
        copy_kernel,
        out_shape=jax.ShapeDtypeStruct(value.shape, value.dtype),
        in_specs=[HBM],
        out_specs=VMEM,
        scratch_shapes=[pltpu.SemaphoreType.DMA],
        compiler_params=PARAMS,
        name="copy_in",
    )(value)


def add_tiles(words, start, stop, unroll, first, held, state, acc, arrive=None):
    last = held.shape[0] - 1

    @pl.loop(0, (stop - start + unroll - 1) // unroll)
    def _(i):
        if arrive is not None:
            arrive(i)
        for u in range(unroll):
            at = start + i * unroll + u
            here = jnp.minimum(at, last)
            word = words[here]
            dst = jnp.where(at < stop, word >> 16, N_SLOT)
            src = jnp.clip(((word >> 8) & 255) - first, 0, state.shape[0] - 1)
            acc[dst] += jnp.dot(held[here], state[src], preferred_element_type=F32)


def load_state(pieces, state):
    for p, piece in enumerate(pieces):
        state[2 * p] = piece[:B]
        state[2 * p + 1] = piece[B:]


def fetch_kernel(words, sizes, tiles, *refs):
    pieces, (acc, held, state, sem) = refs[:5], refs[5:]
    groups = (sizes[1] + GROUP - 1) // GROUP
    early_groups = (sizes[0] + GROUP - 1) // GROUP
    ahead = 4

    def fetch(i):
        for u in range(GROUP):
            at = i * GROUP + u
            pltpu.make_async_copy(tiles.at[words[at] & 255], held.at[at], sem.at[i]).start()

    def arrive(i):
        here = held.at[pl.ds(i * GROUP, GROUP)]
        pltpu.make_async_copy(tiles.at[pl.ds(0, GROUP)], here, sem.at[i]).wait()

    def step(i):
        @pl.when(i + ahead < groups)
        def _():
            fetch(i + ahead)

        arrive(i)

    @pl.loop(0, jnp.minimum(groups, ahead))
    def _(i):
        fetch(i)

    acc[...] = jnp.zeros_like(acc)
    load_state(pieces, state)
    add_tiles(words, 0, sizes[0], GROUP, 0, held, state, acc, step)

    @pl.loop(early_groups, groups)
    def _(i):
        step(i)


def early_kernel(words, sizes, held, *refs):
    pieces, (acc, state) = refs[:5], refs[5:]
    acc[...] = jnp.zeros_like(acc)
    load_state(pieces, state)
    add_tiles(words, 0, sizes[0], GROUP, 0, held, state, acc)


def late_kernel(words, sizes, held, acc, *refs):
    pieces, outs, state = refs[:3], refs[3:7], refs[8]
    load_state(pieces, state)
    add_tiles(words, sizes[0], sizes[1], 8, N_EARLY, held, state, acc)
    for i, out in enumerate(outs):
        for s in range(8):
            out[s] = acc[i * 8 + s].astype(BF)


def tile_sums(words, sizes, tiles, held, early, late):
    acc_type = jax.ShapeDtypeStruct((N_SLOT + 1, B, B), F32)
    n_tiles = tiles.shape[0]
    if held is None:
        acc, held = pl.pallas_call(
            fetch_kernel,
            out_shape=(acc_type, jax.ShapeDtypeStruct(tiles.shape, BF)),
            in_specs=[SMEM, SMEM, HBM] + [VMEM] * len(early),
            out_specs=(VMEM, VMEM),
            scratch_shapes=[
                pltpu.VMEM((N_EARLY, B, B), BF),
                pltpu.SemaphoreType.DMA((n_tiles // GROUP,)),
            ],
            compiler_params=PARAMS,
            cost_estimate=cost(80, 0),
            name="fetch_tiles",
        )(words, sizes, tiles, *early)
    else:
        acc = pl.pallas_call(
            early_kernel,
            out_shape=acc_type,
            in_specs=[SMEM, SMEM] + [VMEM] * (1 + len(early)),
            out_specs=VMEM,
            scratch_shapes=[pltpu.VMEM((N_EARLY, B, B), BF)],
            compiler_params=PARAMS,
            cost_estimate=cost(80, 0),
            name="early_tiles",
        )(words, sizes, held, *early)
    out = jax.ShapeDtypeStruct((8, B, B), BF)
    sums = pl.pallas_call(
        late_kernel,
        out_shape=(out,) * 4 + (acc_type,),
        in_specs=[SMEM, SMEM] + [VMEM] * (2 + len(late)),
        out_specs=(VMEM,) * 5,
        scratch_shapes=[pltpu.VMEM((16 - N_EARLY, B, B), BF)],
        input_output_aliases={3: 4},
        compiler_params=PARAMS,
        cost_estimate=cost(48, 0),
        name="late_tiles",
    )(words, sizes, held, acc, *late)[:4]
    return sums, held


def gather(state):
    far = lax.ppermute(state, "row", X_FAR)
    near = lax.ppermute(state, "row", Y_HI)
    up = lax.ppermute(state, "row", X_UP)
    down = lax.ppermute(state, "row", X_DOWN)
    near_up = lax.ppermute(near, "row", X_UP)
    near_down = lax.ppermute(near, "row", X_DOWN)
    near_far = lax.ppermute(far, "row", Y_HI)
    return (state, near, far, up, down), (near_up, near_down, near_far)


def add(*terms):
    total = terms[0].astype(F32)
    for term in terms[1:]:
        total = total + term.astype(F32)
    return total


def scatter_sum(keep, send):
    other = lax.ppermute(send, "col", CORE)
    far = add(keep[4:6], other[4:6]).astype(BF)
    from_low = lax.ppermute(far[0], "col", Z_UP)
    from_high = lax.ppermute(far[1], "col", Z_DOWN)
    up = jnp.stack([add(keep[2], other[2], from_low), add(keep[3], other[3])]).astype(BF)
    down = jnp.stack([add(keep[6], other[6]), add(keep[7], other[7], from_high)]).astype(BF)
    low = lax.ppermute(up, "col", Z_UP)
    high = lax.ppermute(down, "col", Z_DOWN)
    out = add(keep[1], other[1], low[1], high[1]).astype(BF)
    return keep, other, low, high, lax.ppermute(out, "col", Y_LO)


def update_kernel(flags, weight, inject, state, *refs):
    terms, (new, residual) = refs[:10], refs[10:]
    for k in range(2):
        keep, other, low, high, across = terms[5 * k : 5 * k + 5]
        total = add(keep[0], other[0], low[0], high[0], across[...])
        pre = jnp.dot(total.astype(BF), weight[...], preferred_element_type=F32)
        rows = pl.ds(k * B, B)
        old = state[rows]
        updated = jnp.tanh(pre + inject[rows].astype(F32)).astype(BF)
        updated = jnp.where(flags[k] == 1, old, updated)
        new[rows] = updated
        change = updated.astype(F32) - old.astype(F32)
        residual[k] = jnp.sum(change * change)


def update(flags, weight, inject, state, terms):
    return pl.pallas_call(
        update_kernel,
        out_shape=(
            jax.ShapeDtypeStruct(state.shape, BF),
            jax.ShapeDtypeStruct((2,), F32),
        ),
        in_specs=[SMEM] + [VMEM] * 13,
        out_specs=(VMEM, SMEM),
        compiler_params=PARAMS,
        cost_estimate=cost(2, 0),
        name="update",
    )(flags, weight, inject, state, *terms)


def per_device(features, inject, weight, tiles, tile_rows, tile_cols, tile_count, flags):
    words, sizes = tile_words(tile_rows[0, 0], tile_cols[0, 0], tile_count[0])
    tile_set = pltpu.with_memory_space_constraint(tiles[0, 0], pltpu.HBM)
    state = copy_in(pltpu.with_memory_space_constraint(features, pltpu.HBM))
    held = None
    for step in range(ITERS):
        early, late = gather(state)
        sums, held = tile_sums(words, sizes, tile_set, held, early, late)
        terms = scatter_sum(sums[0], sums[1]) + scatter_sum(sums[2], sums[3])
        state, residual = update(flags, weight, inject, state, terms)
    return state, residual


def solution(mesh):
    in_specs = (
        P(("row", "col"), None),
        P(("row", "col"), None),
        P(),
        P("row", "col", None, None, None),
        P("row", "col", None),
        P("row", "col", None),
        P("row", "col"),
        P(("row", "col")),
    )
    out_specs = (P(("row", "col"), None), P(("row", "col")))
    return jax.shard_map(
        per_device, mesh=mesh, in_specs=in_specs, out_specs=out_specs, check_vma=False
    )
```

time: 145 us -> 125 us (0.86)
  Pallas kernels: 26 us -> 17.6 us
  starting transfers between devices: 60.1 us -> 55.9 us
  waiting for transfers between devices: 47.4 us -> 45.1 us
  matrix products: 2.21 us -> 0 us
  local copies, waits for them, and re-layouts: 1.79 us -> 0.1 us
    ppermute x24 -> x14, starting transfers between devices: 26.4 us -> 13.7 us  [the longest x2 4.9 us: gather(): up = lax.ppermute(state, 'row', X_UP)]
    pallas_call x2 -> x7, Pallas kernels: 26 us -> 17.6 us  [the longest x2 5.04 us: tile_sums(): pl.pallas_call(late_kernel, out_shape=(out,) * 4 + (acc_type,), in_specs=...]
    ppermute x4, starting transfers between devices: 12.9 us -> 21.1 us  [scatter_sum(): from_high = lax.ppermute(far[1], 'col', Z_DOWN)]
    ppermute x4, waiting for transfers between devices: 0.01 us -> 5.81 us  [scatter_sum(): from_low = lax.ppermute(far[0], 'col', Z_UP)]
    ppermute x4, waiting for transfers between devices: 4.51 us -> 0.01 us  [scatter_sum(): high = lax.ppermute(down, 'col', Z_DOWN)]
    ppermute x4 -> x2, waiting for transfers between devices: 4.31 us -> 0.01 us  [gather(): near_down = lax.ppermute(near, 'row', X_DOWN)]
    dot_general x4 -> x0, matrix products: 2.21 us -> none  [per_device(): pre = jnp.dot(aggregate, weight, preferred_element_type=F32)]
    slice x2 -> x0, local copies, waits for them, and re-layouts: 1.69 us -> none  [the longest x1 1.05 us: per_device(): blocks = [features[:B], features[B:]]]
  transfers between devices with their start and end apart: 52 -> 38, of which waited for: 24 -> 15; matrix products, arithmetic and copies ran while one was open for 3% -> 4% of each run, Pallas kernels for 0% -> 7%
where the time goes in v2:
time: 125 us
  starting transfers between devices  55.9 us (45%)
  waiting for transfers between devices  45.1 us (36%)
  Pallas kernels  17.6 us (14%)
  other arithmetic  4.49 us (4%)
  between operations  1.84 us (1%)
    ppermute x4, starting transfers between devices, scatter_sum(): from_high = lax.ppermute(far[1], 'col', Z_DOWN)  21.1 us
    ppermute x4, waiting for transfers between devices, scatter_sum(): low = lax.ppermute(up, 'col', Z_UP)  14.1 us
    ppermute x4, starting transfers between devices, scatter_sum(): high = lax.ppermute(down, 'col', Z_DOWN)  13.1 us
    ppermute x4, waiting for transfers between devices, scatter_sum(): return (keep, other, low, high, lax.ppermute(out, 'col', Y_LO))  9.91 us
    ppermute x2, waiting for transfers between devices, gather(): far = lax.ppermute(state, 'row', X_FAR)  7.34 us
    ppermute x4, waiting for transfers between devices, scatter_sum(): from_low = lax.ppermute(far[0], 'col', Z_UP)  5.81 us
    ppermute x2, starting transfers between devices, gather(): near_up = lax.ppermute(near, 'row', X_UP)  5.61 us
    pallas_call x2, Pallas kernels, tile_sums(): pl.pallas_call(late_kernel, out_shape=(out,) * 4 + (acc_type,), in_specs=...  5.04 us
  transfers between devices with their start and end apart: 38, of which 15 were waited for; matrix products, arithmetic and copies ran while one was open for 4% of the time, Pallas kernels for 7%

profile of v2, /device:TPU:6, one launch (start us, length us, event | category | flops | bytes accessed | tf_op | source)
XLA Modules:
  0.0 125.1 jit_solution(14391361586428343381)
XLA Ops:
  5.1 3.2 %collective-permute-start = (bf16[512,256]{1,0:T(8,128)(2,1)S(1)}, bf16[512,256]{1,0:T(8,128)(2,1)S(1)}, u32[]{:S(2)}, u32[]{:S(2)}) collective-permute-start(bf16[512,256]{1,0:T(8,128)(2,1)S(1)} %copy_in.1.refs_0_.state), channel_id=1, source_target_pairs={{0,16},{16,0},{32,48},{48,32},{64,80},{80,64},{96,112},{112,96},{1... | collective-permute-start | bytes 786440 | tf_op jit(solution)/shard_map/ppermute | solution.py:213
  11.2 2.7 %collective-permute-done.refs_1_ = bf16[512,256]{1,0:T(8,128)(2,1)S(1)} collective-permute-done((bf16[512,256]{1,0:T(8,128)(2,1)S(1)}, bf16[512,256]{1,0:T(8,128)(2,1)S(1)}, u32[]{:S(2)}, u32[]{:S(2)}) %collective-permute-start) | collective-permute-done | bytes 262176 | tf_op jit(solution)/shard_map/ppermute | solution.py:213
  17.1 3.2 %collective-permute-start.6 = (bf16[512,256]{1,0:T(8,128)(2,1)S(1)}, bf16[512,256]{1,0:T(8,128)(2,1)S(1)}, u32[]{:S(2)}, u32[]{:S(2)}) collective-permute-start(bf16[512,256]{1,0:T(8,128)(2,1)S(1)} %collective-permute-done.1.refs_2_), channel_id=1, source_target_pairs={{0,16},{16,0},{32,48},{48,32},{64,80},{80,64},{96,112},{112,96},{1... | collective-permute-start | bytes 786440 | tf_op jit(solution)/shard_map/ppermute | solution.py:218
  21.1 4.8 %fetch_tiles.1 = (f32[33,256,256]{2,1,0:T(8,128)S(1)}, bf16[128,256,256]{2,1,0:T(8,128)(2,1)S(1)}) custom-call(s32[128]{0:T(128)S(1)} %select_reduce_fusion.words, s32[2]{0:T(128)S(1)} %pad_add_fusion.sizes, bf16[128,256,256]{2,1,0:T(8,128)(2,1)} %bitcast.107, bf16[512,256]{1,0:T(8,128)(2,1)S(1)} %copy_in.1.refs_0_.state, ...), custom_call_target="tpu_custom_call" | custom-call | flops 2684354560 | tf_op jit(solution)/shard_map/fetch_tiles/pallas_call | solution.py:172
  25.9 2.5 %late_tiles.2 = (bf16[8,256,256]{2,1,0:T(8,128)(2,1)S(1)}, bf16[8,256,256]{2,1,0:T(8,128)(2,1)S(1)}, bf16[8,256,256]{2,1,0:T(8,128)(2,1)S(1)}, bf16[8,256,256]{2,1,0:T(8,128)(2,1)S(1)}, f32[33,256,256]{2,1,0:T(8,128)S(1)}) custom-call(s32[128]{0:T(128)S(1)} %select_reduce_fusion.words, s32[2]{0:T(128)S(1)} %pad_add_fusion.sizes, ...), custom_call_target="tpu_custom_call", output_to_operand_aliasing={{4}: (3, {})} | custom-call | flops 1610612736 | tf_op jit(solution)/shard_map/late_tiles/pallas_call | solution.py:197
  31.3 8.3 %collective-permute-start.10 = (bf16[256,256]{1,0:T(8,128)(2,1)S(1)}, bf16[256,256]{1,0:T(8,128)(2,1)S(1)}, u32[]{:S(2)}, u32[]{:S(2)}) collective-permute-start(bf16[256,256]{1,0:T(8,128)(2,1)S(1)} %get-tuple-element.48), channel_id=1, source_target_pairs={{0,6},{1,7},{2,0},{3,1},{4,2},{5,3},{6,4},{7,5},{8,14},{9,15},{10,... | collective-permute-start | bytes 393224 | tf_op jit(solution)/shard_map/ppermute | solution.py:233
  39.7 3.3 %collective-permute-start.16 = (bf16[256,256]{1,0:T(8,128)(2,1)S(1)}, bf16[256,256]{1,0:T(8,128)(2,1)S(1)}, u32[]{:S(2)}, u32[]{:S(2)}) collective-permute-start(bf16[256,256]{1,0:T(8,128)(2,1)S(1)} %get-tuple-element.46), channel_id=1, source_target_pairs={{0,6},{1,7},{2,0},{3,1},{4,2},{5,3},{6,4},{7,5},{8,14},{9,15},{10,... | collective-permute-start | bytes 393224 | tf_op jit(solution)/shard_map/ppermute | solution.py:233
  43.2 2.9 %collective-permute-done.8 = bf16[256,256]{1,0:T(8,128)(2,1)S(1)} collective-permute-done((bf16[256,256]{1,0:T(8,128)(2,1)S(1)}, bf16[256,256]{1,0:T(8,128)(2,1)S(1)}, u32[]{:S(2)}, u32[]{:S(2)}) %collective-permute-start.8) | collective-permute-done | bytes 131104 | tf_op jit(solution)/shard_map/ppermute | solution.py:232
  46.3 3.3 %collective-permute-start.11 = (bf16[2,256,256]{2,1,0:T(8,128)(2,1)S(1)}, bf16[2,256,256]{2,1,0:T(8,128)(2,1)S(1)}, u32[]{:S(2)}, u32[]{:S(2)}) collective-permute-start(bf16[2,256,256]{2,1,0:T(8,128)(2,1)S(1)} %pad_maximum_fusion.1), channel_id=1, source_target_pairs={{0,6},{1,7},{2,0},{3,1},{4,2},{5,3},{6,4},{7,5},{8,14},{9,15},{10,... | collective-permute-start | bytes 786440 | tf_op jit(solution)/shard_map/ppermute | solution.py:237
  49.9 3.3 %collective-permute-start.17 = (bf16[2,256,256]{2,1,0:T(8,128)(2,1)S(1)}, bf16[2,256,256]{2,1,0:T(8,128)(2,1)S(1)}, u32[]{:S(2)}, u32[]{:S(2)}) collective-permute-start(bf16[2,256,256]{2,1,0:T(8,128)(2,1)S(1)} %pad_maximum_fusion.3), channel_id=1, source_target_pairs={{0,6},{1,7},{2,0},{3,1},{4,2},{5,3},{6,4},{7,5},{8,14},{9,15},{10,... | collective-permute-start | bytes 786440 | tf_op jit(solution)/shard_map/ppermute | solution.py:237
  53.2 3.6 %collective-permute-done.9.refs_2_ = bf16[2,256,256]{2,1,0:T(8,128)(2,1)S(1)} collective-permute-done((bf16[2,256,256]{2,1,0:T(8,128)(2,1)S(1)}, bf16[2,256,256]{2,1,0:T(8,128)(2,1)S(1)}, u32[]{:S(2)}, u32[]{:S(2)}) %collective-permute-start.9) | collective-permute-done | bytes 262176 | tf_op jit(solution)/shard_map/ppermute | solution.py:236
  56.9 3.5 %collective-permute-done.15.refs_7_ = bf16[2,256,256]{2,1,0:T(8,128)(2,1)S(1)} collective-permute-done((bf16[2,256,256]{2,1,0:T(8,128)(2,1)S(1)}, bf16[2,256,256]{2,1,0:T(8,128)(2,1)S(1)}, u32[]{:S(2)}, u32[]{:S(2)}) %collective-permute-start.15) | collective-permute-done | bytes 262176 | tf_op jit(solution)/shard_map/ppermute | solution.py:236
  62.4 3.2 %collective-permute-done.18.refs_9_ = bf16[256,256]{1,0:T(8,128)(2,1)S(1)} collective-permute-done((bf16[256,256]{1,0:T(8,128)(2,1)S(1)}, bf16[256,256]{1,0:T(8,128)(2,1)S(1)}, u32[]{:S(2)}, u32[]{:S(2)}) %collective-permute-start.18) | collective-permute-done | bytes 131104 | tf_op jit(solution)/shard_map/ppermute | solution.py:239
  70.6 7.3 %collective-permute-done.20.refs_2_ = bf16[512,256]{1,0:T(8,128)(2,1)S(1)} collective-permute-done((bf16[512,256]{1,0:T(8,128)(2,1)S(1)}, bf16[512,256]{1,0:T(8,128)(2,1)S(1)}, u32[]{:S(2)}, u32[]{:S(2)}) %collective-permute-start.20) | collective-permute-done | bytes 262176 | tf_op jit(solution)/shard_map/ppermute | solution.py:212
  78.0 3.2 %collective-permute-start.23 = (bf16[512,256]{1,0:T(8,128)(2,1)S(1)}, bf16[512,256]{1,0:T(8,128)(2,1)S(1)}, u32[]{:S(2)}, u32[]{:S(2)}) collective-permute-start(bf16[512,256]{1,0:T(8,128)(2,1)S(1)} %collective-permute-done.19.refs_1_), channel_id=1, source_target_pairs={{0,32},{16,48},{32,64},{48,80},{64,96},{80,112},{96,0},{112,16},{1... | collective-permute-start | bytes 786440 | tf_op jit(solution)/shard_map/ppermute | solution.py:216
  81.2 3.7 %early_tiles.1.acc = f32[33,256,256]{2,1,0:T(8,128)S(1)} custom-call(s32[128]{0:T(128)S(1)} %select_reduce_fusion.words, s32[2]{0:T(128)S(1)} %pad_add_fusion.sizes, bf16[128,256,256]{2,1,0:T(8,128)(2,1)S(1)} %get-tuple-element.13.held, bf16[512,256]{1,0:T(8,128)(2,1)S(1)} %get-tuple-element.19.refs_0_.state, ...), custom_call_target="tpu_custom_call" | custom-call | flops 2684354560 | tf_op jit(solution)/shard_map/early_tiles/pallas_call | solution.py:186
  91.2 6.2 %collective-permute-start.29 = (bf16[256,256]{1,0:T(8,128)(2,1)S(1)}, bf16[256,256]{1,0:T(8,128)(2,1)S(1)}, u32[]{:S(2)}, u32[]{:S(2)}) collective-permute-start(bf16[256,256]{1,0:T(8,128)(2,1)S(1)} %get-tuple-element.44), channel_id=1, source_target_pairs={{0,6},{1,7},{2,0},{3,1},{4,2},{5,3},{6,4},{7,5},{8,14},{9,15},{10,... | collective-permute-start | bytes 393224 | tf_op jit(solution)/shard_map/ppermute | solution.py:233
  97.5 3.3 %collective-permute-start.35 = (bf16[256,256]{1,0:T(8,128)(2,1)S(1)}, bf16[256,256]{1,0:T(8,128)(2,1)S(1)}, u32[]{:S(2)}, u32[]{:S(2)}) collective-permute-start(bf16[256,256]{1,0:T(8,128)(2,1)S(1)} %get-tuple-element.42), channel_id=1, source_target_pairs={{0,6},{1,7},{2,0},{3,1},{4,2},{5,3},{6,4},{7,5},{8,14},{9,15},{10,... | collective-permute-start | bytes 393224 | tf_op jit(solution)/shard_map/ppermute | solution.py:233
  101.0 2.9 %collective-permute-done.27 = bf16[256,256]{1,0:T(8,128)(2,1)S(1)} collective-permute-done((bf16[256,256]{1,0:T(8,128)(2,1)S(1)}, bf16[256,256]{1,0:T(8,128)(2,1)S(1)}, u32[]{:S(2)}, u32[]{:S(2)}) %collective-permute-start.27) | collective-permute-done | bytes 131104 | tf_op jit(solution)/shard_map/ppermute | solution.py:232
  104.1 3.3 %collective-permute-start.30 = (bf16[2,256,256]{2,1,0:T(8,128)(2,1)S(1)}, bf16[2,256,256]{2,1,0:T(8,128)(2,1)S(1)}, u32[]{:S(2)}, u32[]{:S(2)}) collective-permute-start(bf16[2,256,256]{2,1,0:T(8,128)(2,1)S(1)} %pad_maximum_fusion.5), channel_id=1, source_target_pairs={{0,6},{1,7},{2,0},{3,1},{4,2},{5,3},{6,4},{7,5},{8,14},{9,15},{10,... | collective-permute-start | bytes 786440 | tf_op jit(solution)/shard_map/ppermute | solution.py:237
  107.7 3.3 %collective-permute-start.36 = (bf16[2,256,256]{2,1,0:T(8,128)(2,1)S(1)}, bf16[2,256,256]{2,1,0:T(8,128)(2,1)S(1)}, u32[]{:S(2)}, u32[]{:S(2)}) collective-permute-start(bf16[2,256,256]{2,1,0:T(8,128)(2,1)S(1)} %pad_maximum_fusion.7), channel_id=1, source_target_pairs={{0,6},{1,7},{2,0},{3,1},{4,2},{5,3},{6,4},{7,5},{8,14},{9,15},{10,... | collective-permute-start | bytes 786440 | tf_op jit(solution)/shard_map/ppermute | solution.py:237
  111.0 3.6 %collective-permute-done.28.refs_2_ = bf16[2,256,256]{2,1,0:T(8,128)(2,1)S(1)} collective-permute-done((bf16[2,256,256]{2,1,0:T(8,128)(2,1)S(1)}, bf16[2,256,256]{2,1,0:T(8,128)(2,1)S(1)}, u32[]{:S(2)}, u32[]{:S(2)}) %collective-permute-start.28) | collective-permute-done | bytes 262176 | tf_op jit(solution)/shard_map/ppermute | solution.py:236
  114.7 3.5 %collective-permute-done.34.refs_7_ = bf16[2,256,256]{2,1,0:T(8,128)(2,1)S(1)} collective-permute-done((bf16[2,256,256]{2,1,0:T(8,128)(2,1)S(1)}, bf16[2,256,256]{2,1,0:T(8,128)(2,1)S(1)}, u32[]{:S(2)}, u32[]{:S(2)}) %collective-permute-start.34) | collective-permute-done | bytes 262176 | tf_op jit(solution)/shard_map/ppermute | solution.py:236
  120.2 3.1 %collective-permute-done.37.refs_9_ = bf16[256,256]{1,0:T(8,128)(2,1)S(1)} collective-permute-done((bf16[256,256]{1,0:T(8,128)(2,1)S(1)}, bf16[256,256]{1,0:T(8,128)(2,1)S(1)}, u32[]{:S(2)}, u32[]{:S(2)}) %collective-permute-start.37) | collective-permute-done | bytes 131104 | tf_op jit(solution)/shard_map/ppermute | solution.py:239
  (98 shorter events, 32.1 us)
Async XLA Ops:
  1.6 19.5 %collective-permute-start.3 = (bf16[512,256]{1,0:T(8,128)(2,1)S(1)}, bf16[512,256]{1,0:T(8,128)(2,1)S(1)}, u32[]{:S(2)}, u32[]{:S(2)}) collective-permute-start(bf16[512,256]{1,0:T(8,128)(2,1)S(1)} %copy_in.1.refs_0_.state), channel_id=1, source_target_pairs={{0,96},{16,112},{32,0},{48,16},{64,32},{80,48},{96,64},{112,80},{1... | collective-permute-start | bytes 786440 | tf_op jit(solution)/shard_map/ppermute | solution.py:215
  2.5 18.6 %collective-permute-start.2 = (bf16[512,256]{1,0:T(8,128)(2,1)S(1)}, bf16[512,256]{1,0:T(8,128)(2,1)S(1)}, u32[]{:S(2)}, u32[]{:S(2)}) collective-permute-start(bf16[512,256]{1,0:T(8,128)(2,1)S(1)} %copy_in.1.refs_0_.state), channel_id=1, source_target_pairs={{0,32},{16,48},{32,64},{48,80},{64,96},{80,112},{96,0},{112,16},{1... | collective-permute-start | bytes 786440 | tf_op jit(solution)/shard_map/ppermute | solution.py:214
  4.9 12.2 %collective-permute-start.1 = (bf16[512,256]{1,0:T(8,128)(2,1)S(1)}, bf16[512,256]{1,0:T(8,128)(2,1)S(1)}, u32[]{:S(2)}, u32[]{:S(2)}) collective-permute-start(bf16[512,256]{1,0:T(8,128)(2,1)S(1)} %copy_in.1.refs_0_.state), channel_id=1, source_target_pairs={{0,64},{16,80},{32,96},{48,112},{64,0},{80,16},{96,32},{112,48},{1... | collective-permute-start | bytes 786440 | tf_op jit(solution)/shard_map/ppermute | solution.py:212
  5.1 8.8 %collective-permute-start = (bf16[512,256]{1,0:T(8,128)(2,1)S(1)}, bf16[512,256]{1,0:T(8,128)(2,1)S(1)}, u32[]{:S(2)}, u32[]{:S(2)}) collective-permute-start(bf16[512,256]{1,0:T(8,128)(2,1)S(1)} %copy_in.1.refs_0_.state), channel_id=1, source_target_pairs={{0,16},{16,0},{32,48},{48,32},{64,80},{80,64},{96,112},{112,96},{1... | collective-permute-start | bytes 786440 | tf_op jit(solution)/shard_map/ppermute | solution.py:213
  13.9 12.0 %collective-permute-start.5 = (bf16[512,256]{1,0:T(8,128)(2,1)S(1)}, bf16[512,256]{1,0:T(8,128)(2,1)S(1)}, u32[]{:S(2)}, u32[]{:S(2)}) collective-permute-start(bf16[512,256]{1,0:T(8,128)(2,1)S(1)} %collective-permute-done.refs_1_), channel_id=1, source_target_pairs={{0,96},{16,112},{32,0},{48,16},{64,32},{80,48},{96,64},{112,80},{1... | collective-permute-start | bytes 786440 | tf_op jit(solution)/shard_map/ppermute | solution.py:217
  14.8 11.1 %collective-permute-start.4 = (bf16[512,256]{1,0:T(8,128)(2,1)S(1)}, bf16[512,256]{1,0:T(8,128)(2,1)S(1)}, u32[]{:S(2)}, u32[]{:S(2)}) collective-permute-start(bf16[512,256]{1,0:T(8,128)(2,1)S(1)} %collective-permute-done.refs_1_), channel_id=1, source_target_pairs={{0,32},{16,48},{32,64},{48,80},{64,96},{80,112},{96,0},{112,16},{1... | collective-permute-start | bytes 786440 | tf_op jit(solution)/shard_map/ppermute | solution.py:216
  28.6 11.1 %collective-permute-start.13 = (bf16[8,256,256]{2,1,0:T(8,128)(2,1)S(1)}, bf16[8,256,256]{2,1,0:T(8,128)(2,1)S(1)}, u32[]{:S(2)}, u32[]{:S(2)}) collective-permute-start(bf16[8,256,256]{2,1,0:T(8,128)(2,1)S(1)} %get-tuple-element.18), channel_id=1, source_target_pairs={{0,1},{1,0},{2,3},{3,2},{4,5},{5,4},{6,7},{7,6},{8,9},{9,8},{10,11... | collective-permute-start | bytes 3145736 | tf_op jit(solution)/shard_map/ppermute | solution.py:230
  31.3 11.9 %collective-permute-start.10 = (bf16[256,256]{1,0:T(8,128)(2,1)S(1)}, bf16[256,256]{1,0:T(8,128)(2,1)S(1)}, u32[]{:S(2)}, u32[]{:S(2)}) collective-permute-start(bf16[256,256]{1,0:T(8,128)(2,1)S(1)} %get-tuple-element.48), channel_id=1, source_target_pairs={{0,6},{1,7},{2,0},{3,1},{4,2},{5,3},{6,4},{7,5},{8,14},{9,15},{10,... | collective-permute-start | bytes 393224 | tf_op jit(solution)/shard_map/ppermute | solution.py:233
  39.7 9.9 %collective-permute-start.16 = (bf16[256,256]{1,0:T(8,128)(2,1)S(1)}, bf16[256,256]{1,0:T(8,128)(2,1)S(1)}, u32[]{:S(2)}, u32[]{:S(2)}) collective-permute-start(bf16[256,256]{1,0:T(8,128)(2,1)S(1)} %get-tuple-element.46), channel_id=1, source_target_pairs={{0,6},{1,7},{2,0},{3,1},{4,2},{5,3},{6,4},{7,5},{8,14},{9,15},{10,... | collective-permute-start | bytes 393224 | tf_op jit(solution)/shard_map/ppermute | solution.py:233
  46.2 10.5 %collective-permute-start.9 = (bf16[2,256,256]{2,1,0:T(8,128)(2,1)S(1)}, bf16[2,256,256]{2,1,0:T(8,128)(2,1)S(1)}, u32[]{:S(2)}, u32[]{:S(2)}) collective-permute-start(bf16[2,256,256]{2,1,0:T(8,128)(2,1)S(1)} %pad_maximum_fusion), channel_id=1, source_target_pairs={{0,2},{1,3},{2,4},{3,5},{4,6},{5,7},{6,0},{7,1},{8,10},{9,11},{10,... | collective-permute-start | bytes 786440 | tf_op jit(solution)/shard_map/ppermute | solution.py:236
  46.3 10.4 %collective-permute-start.11 = (bf16[2,256,256]{2,1,0:T(8,128)(2,1)S(1)}, bf16[2,256,256]{2,1,0:T(8,128)(2,1)S(1)}, u32[]{:S(2)}, u32[]{:S(2)}) collective-permute-start(bf16[2,256,256]{2,1,0:T(8,128)(2,1)S(1)} %pad_maximum_fusion.1), channel_id=1, source_target_pairs={{0,6},{1,7},{2,0},{3,1},{4,2},{5,3},{6,4},{7,5},{8,14},{9,15},{10,... | collective-permute-start | bytes 786440 | tf_op jit(solution)/shard_map/ppermute | solution.py:237
  49.8 10.6 %collective-permute-start.15 = (bf16[2,256,256]{2,1,0:T(8,128)(2,1)S(1)}, bf16[2,256,256]{2,1,0:T(8,128)(2,1)S(1)}, u32[]{:S(2)}, u32[]{:S(2)}) collective-permute-start(bf16[2,256,256]{2,1,0:T(8,128)(2,1)S(1)} %pad_maximum_fusion.2), channel_id=1, source_target_pairs={{0,2},{1,3},{2,4},{3,5},{4,6},{5,7},{6,0},{7,1},{8,10},{9,11},{10,... | collective-permute-start | bytes 786440 | tf_op jit(solution)/shard_map/ppermute | solution.py:236
  49.9 10.5 %collective-permute-start.17 = (bf16[2,256,256]{2,1,0:T(8,128)(2,1)S(1)}, bf16[2,256,256]{2,1,0:T(8,128)(2,1)S(1)}, u32[]{:S(2)}, u32[]{:S(2)}) collective-permute-start(bf16[2,256,256]{2,1,0:T(8,128)(2,1)S(1)} %pad_maximum_fusion.3), channel_id=1, source_target_pairs={{0,6},{1,7},{2,0},{3,1},{4,2},{5,3},{6,4},{7,5},{8,14},{9,15},{10,... | collective-permute-start | bytes 786440 | tf_op jit(solution)/shard_map/ppermute | solution.py:237
  67.1 10.8 %collective-permute-start.20 = (bf16[512,256]{1,0:T(8,128)(2,1)S(1)}, bf16[512,256]{1,0:T(8,128)(2,1)S(1)}, u32[]{:S(2)}, u32[]{:S(2)}) collective-permute-start(bf16[512,256]{1,0:T(8,128)(2,1)S(1)} %get-tuple-element.19.refs_0_.state), channel_id=1, source_target_pairs={{0,64},{16,80},{32,96},{48,112},{64,0},{80,16},{96,32},{112,48},{1... | collective-permute-start | bytes 786440 | tf_op jit(solution)/shard_map/ppermute | solution.py:212
  67.2 10.7 %collective-permute-start.19 = (bf16[512,256]{1,0:T(8,128)(2,1)S(1)}, bf16[512,256]{1,0:T(8,128)(2,1)S(1)}, u32[]{:S(2)}, u32[]{:S(2)}) collective-permute-start(bf16[512,256]{1,0:T(8,128)(2,1)S(1)} %get-tuple-element.19.refs_0_.state), channel_id=1, source_target_pairs={{0,16},{16,0},{32,48},{48,32},{64,80},{80,64},{96,112},{112,96},{1... | collective-permute-start | bytes 786440 | tf_op jit(solution)/shard_map/ppermute | solution.py:213
  67.3 13.8 %collective-permute-start.22 = (bf16[512,256]{1,0:T(8,128)(2,1)S(1)}, bf16[512,256]{1,0:T(8,128)(2,1)S(1)}, u32[]{:S(2)}, u32[]{:S(2)}) collective-permute-start(bf16[512,256]{1,0:T(8,128)(2,1)S(1)} %get-tuple-element.19.refs_0_.state), channel_id=1, source_target_pairs={{0,96},{16,112},{32,0},{48,16},{64,32},{80,48},{96,64},{112,80},{1... | collective-permute-start | bytes 786440 | tf_op jit(solution)/shard_map/ppermute | solution.py:215
  68.1 13.1 %collective-permute-start.21 = (bf16[512,256]{1,0:T(8,128)(2,1)S(1)}, bf16[512,256]{1,0:T(8,128)(2,1)S(1)}, u32[]{:S(2)}, u32[]{:S(2)}) collective-permute-start(bf16[512,256]{1,0:T(8,128)(2,1)S(1)} %get-tuple-element.19.refs_0_.state), channel_id=1, source_target_pairs={{0,32},{16,48},{32,64},{48,80},{64,96},{80,112},{96,0},{112,16},{1... | collective-permute-start | bytes 786440 | tf_op jit(solution)/shard_map/ppermute | solution.py:214
  88.4 9.0 %collective-permute-start.32 = (bf16[8,256,256]{2,1,0:T(8,128)(2,1)S(1)}, bf16[8,256,256]{2,1,0:T(8,128)(2,1)S(1)}, u32[]{:S(2)}, u32[]{:S(2)}) collective-permute-start(bf16[8,256,256]{2,1,0:T(8,128)(2,1)S(1)} %get-tuple-element.23), channel_id=1, source_target_pairs={{0,1},{1,0},{2,3},{3,2},{4,5},{5,4},{6,7},{7,6},{8,9},{9,8},{10,11... | collective-permute-start | bytes 3145736 | tf_op jit(solution)/shard_map/ppermute | solution.py:230
  91.2 9.8 %collective-permute-start.29 = (bf16[256,256]{1,0:T(8,128)(2,1)S(1)}, bf16[256,256]{1,0:T(8,128)(2,1)S(1)}, u32[]{:S(2)}, u32[]{:S(2)}) collective-permute-start(bf16[256,256]{1,0:T(8,128)(2,1)S(1)} %get-tuple-element.44), channel_id=1, source_target_pairs={{0,6},{1,7},{2,0},{3,1},{4,2},{5,3},{6,4},{7,5},{8,14},{9,15},{10,... | collective-permute-start | bytes 393224 | tf_op jit(solution)/shard_map/ppermute | solution.py:233
  97.5 9.9 %collective-permute-start.35 = (bf16[256,256]{1,0:T(8,128)(2,1)S(1)}, bf16[256,256]{1,0:T(8,128)(2,1)S(1)}, u32[]{:S(2)}, u32[]{:S(2)}) collective-permute-start(bf16[256,256]{1,0:T(8,128)(2,1)S(1)} %get-tuple-element.42), channel_id=1, source_target_pairs={{0,6},{1,7},{2,0},{3,1},{4,2},{5,3},{6,4},{7,5},{8,14},{9,15},{10,... | collective-permute-start | bytes 393224 | tf_op jit(solution)/shard_map/ppermute | solution.py:233
  104.0 10.5 %collective-permute-start.28 = (bf16[2,256,256]{2,1,0:T(8,128)(2,1)S(1)}, bf16[2,256,256]{2,1,0:T(8,128)(2,1)S(1)}, u32[]{:S(2)}, u32[]{:S(2)}) collective-permute-start(bf16[2,256,256]{2,1,0:T(8,128)(2,1)S(1)} %pad_maximum_fusion.4), channel_id=1, source_target_pairs={{0,2},{1,3},{2,4},{3,5},{4,6},{5,7},{6,0},{7,1},{8,10},{9,11},{10,... | collective-permute-start | bytes 786440 | tf_op jit(solution)/shard_map/ppermute | solution.py:236
  104.1 10.4 %collective-permute-start.30 = (bf16[2,256,256]{2,1,0:T(8,128)(2,1)S(1)}, bf16[2,256,256]{2,1,0:T(8,128)(2,1)S(1)}, u32[]{:S(2)}, u32[]{:S(2)}) collective-permute-start(bf16[2,256,256]{2,1,0:T(8,128)(2,1)S(1)} %pad_maximum_fusion.5), channel_id=1, source_target_pairs={{0,6},{1,7},{2,0},{3,1},{4,2},{5,3},{6,4},{7,5},{8,14},{9,15},{10,... | collective-permute-start | bytes 786440 | tf_op jit(solution)/shard_map/ppermute | solution.py:237
  107.6 10.7 %collective-permute-start.34 = (bf16[2,256,256]{2,1,0:T(8,128)(2,1)S(1)}, bf16[2,256,256]{2,1,0:T(8,128)(2,1)S(1)}, u32[]{:S(2)}, u32[]{:S(2)}) collective-permute-start(bf16[2,256,256]{2,1,0:T(8,128)(2,1)S(1)} %pad_maximum_fusion.6), channel_id=1, source_target_pairs={{0,2},{1,3},{2,4},{3,5},{4,6},{5,7},{6,0},{7,1},{8,10},{9,11},{10,... | collective-permute-start | bytes 786440 | tf_op jit(solution)/shard_map/ppermute | solution.py:236
  107.7 10.5 %collective-permute-start.36 = (bf16[2,256,256]{2,1,0:T(8,128)(2,1)S(1)}, bf16[2,256,256]{2,1,0:T(8,128)(2,1)S(1)}, u32[]{:S(2)}, u32[]{:S(2)}) collective-permute-start(bf16[2,256,256]{2,1,0:T(8,128)(2,1)S(1)} %pad_maximum_fusion.7), channel_id=1, source_target_pairs={{0,6},{1,7},{2,0},{3,1},{4,2},{5,3},{6,4},{7,5},{8,14},{9,15},{10,... | collective-permute-start | bytes 786440 | tf_op jit(solution)/shard_map/ppermute | solution.py:237
  (17 other events, 196.6 us)

commit v3 on v2

v3 whole, which is shorter than its diff:
```python
import functools

import jax
import jax.numpy as jnp
from jax import lax
from jax.experimental import pallas as pl
from jax.experimental.pallas import tpu as pltpu
from jax.sharding import PartitionSpec as P

ITERS = 2
B = 256
BF = jnp.bfloat16
F32 = jnp.float32
N_SLOT = 32
FIRST = (0, 6, 10, 16)
GROUP = 16
VMEM_LIMIT = 16 * 2**20
PIECES = (0, 1, 4, 6, 2, 7, 3, 5)


def col_perm(f):
    pairs = []
    for i in range(16):
        y, z, c = f(i // 8, i // 2 % 4, i % 2)
        pairs.append((i, (y % 2) * 8 + (z % 4) * 2 + c % 2))
    return pairs


def row_perm(f):
    pairs = []
    for i in range(8):
        x, y = f(i // 2, i % 2)
        pairs.append((i, (x % 4) * 2 + y % 2))
    return pairs


CORE = col_perm(lambda y, z, c: (y, z, c + 1))
Z_UP = col_perm(lambda y, z, c: (y, z + 1, c))
Z_DOWN = col_perm(lambda y, z, c: (y, z - 1, c))
Z_FAR = col_perm(lambda y, z, c: (y, z + 2, c))
Y_LO = col_perm(lambda y, z, c: (y + 1, z, c))
Y_HI = row_perm(lambda x, y: (x, y + 1))
X_UP = row_perm(lambda x, y: (x + 1, y))
X_DOWN = row_perm(lambda x, y: (x - 1, y))
X_FAR = row_perm(lambda x, y: (x + 2, y))


SMEM = pl.BlockSpec(memory_space=pltpu.SMEM)
VMEM = pl.BlockSpec(memory_space=pltpu.VMEM)
HBM = pl.BlockSpec(memory_space=pltpu.HBM)
PARAMS = pltpu.CompilerParams(vmem_limit_bytes=VMEM_LIMIT)


def cost(n_tiles, extra):
    return pl.CostEstimate(
        flops=n_tiles * 2 * B**3, bytes_accessed=extra, transcendentals=0
    )


def prepare_kernel(row_list, col_list, count, features, table, state, rows, cols, sem):
    copies = [
        pltpu.make_async_copy(source, target, sem.at[s])
        for s, (source, target) in enumerate(
            ((row_list, rows), (col_list, cols), (features, state))
        )
    ]
    for copy in copies:
        copy.start()
    copies[0].wait()
    copies[1].wait()
    row, col = lax.axis_index("row"), lax.axis_index("col")
    x, yh = row >> 1, row & 1
    yl, z, core = col >> 3, (col >> 1) & 3, col & 1
    n = rows.shape[1]
    i, j = rows[...], cols[...]
    dy = (i >> 4) ^ yl
    half = ((i >> 1) & 1) ^ core
    dst = dy * 16 + half * 8 + (((i >> 2) - z) & 3) * 2 + (i & 1)
    place = (((j >> 2) - x) & 3) * 2 + (((j >> 1) & 1) ^ yh)
    src = jnp.zeros_like(place)
    for at, piece in enumerate(PIECES):
        src = jnp.where(place == at, piece, src)
    src = src * 2 + (j & 1)
    index = lax.broadcasted_iota(jnp.int32, (1, n), 1)
    kind = jnp.where(src < FIRST[1], 0, jnp.where(src < FIRST[2], 1, 3 - dy))
    kind = jnp.where(index < count[0], kind, 4)
    word = index + src * 256 + dst * 65536
    key = jnp.broadcast_to((kind * 256 + index).astype(F32), (n, n))
    rank = jnp.sum((key < key.T).astype(F32), axis=1, keepdims=True)
    slot = lax.broadcasted_iota(jnp.int32, (n, n), 1).astype(F32)
    listed = jnp.broadcast_to(word.astype(F32), (n, n)).T
    words = jnp.sum(jnp.where(rank == slot, listed, 0.0), axis=0, keepdims=True)
    ends = jnp.zeros((1, n), F32)
    for k in range(4):
        end = jnp.sum((kind <= k).astype(F32), axis=1, keepdims=True)
        ends = jnp.where(index == k, end, ends)
    table[0:1, :] = words.astype(jnp.int32)
    table[1:2, :] = ends.astype(jnp.int32)
    copies[2].wait()


def prepare(rows, cols, count, features):
    return pl.pallas_call(
        prepare_kernel,
        out_shape=(
            jax.ShapeDtypeStruct((2, rows.shape[1]), jnp.int32),
            jax.ShapeDtypeStruct(features.shape, features.dtype),
        ),
        in_specs=[HBM, HBM, SMEM, HBM],
        out_specs=(VMEM, VMEM),
        scratch_shapes=[pltpu.VMEM(rows.shape, jnp.int32)] * 2 + [pltpu.SemaphoreType.DMA((3,))],
        compiler_params=PARAMS,
        cost_estimate=cost(0, 0),
        name="prepare",
    )(rows, cols, count, features)


def add_tiles(table, start, stop, unroll, first, held, state, acc, arrive=None):
    last = held.shape[0] - 1

    @pl.loop(0, (stop - start + unroll - 1) // unroll)
    def _(i):
        if arrive is not None:
            arrive(i)
        for u in range(unroll):
            at = start + i * unroll + u
            here = jnp.minimum(at, last)
            word = table[0, here]
            dst = jnp.where(at < stop, word >> 16, N_SLOT)
            src = jnp.clip(((word >> 8) & 255) - first, 0, state.shape[0] - 1)
            acc[dst] += jnp.dot(held[here], state[src], preferred_element_type=F32)


def load_state(pieces, state):
    for p, piece in enumerate(pieces):
        state[2 * p] = piece[:B]
        state[2 * p + 1] = piece[B:]


def fetch_kernel(table, tiles, *refs):
    pieces, (acc, held, state, sem) = refs[:3], refs[3:]
    groups = (table[1, 3] + GROUP - 1) // GROUP
    first_groups = (table[1, 0] + GROUP - 1) // GROUP
    ahead = 4

    def fetch(i):
        for u in range(GROUP):
            at = i * GROUP + u
            pltpu.make_async_copy(tiles.at[table[0, at] & 255], held.at[at], sem.at[i]).start()

    def step(i):
        @pl.when(i + ahead < groups)
        def _():
            fetch(i + ahead)

        here = held.at[pl.ds(i * GROUP, GROUP)]
        pltpu.make_async_copy(tiles.at[pl.ds(0, GROUP)], here, sem.at[i]).wait()

    @pl.loop(0, jnp.minimum(groups, ahead))
    def _(i):
        fetch(i)

    acc[...] = jnp.zeros_like(acc)
    load_state(pieces, state)
    add_tiles(table, 0, table[1, 0], GROUP, FIRST[0], held, state, acc, step)

    @pl.loop(first_groups, groups)
    def _(i):
        step(i)


def first_kernel(table, held, *refs):
    pieces, (acc, state) = refs[:3], refs[3:]
    acc[...] = jnp.zeros_like(acc)
    load_state(pieces, state)
    add_tiles(table, 0, table[1, 0], GROUP, FIRST[0], held, state, acc)


def second_kernel(table, held, acc, *refs):
    pieces, state = refs[:2], refs[3]
    load_state(pieces, state)
    add_tiles(table, table[1, 0], table[1, 1], 8, FIRST[1], held, state, acc)


def late_kernel(dy, table, held, acc, *refs):
    pieces, outs, state = refs[:3], refs[3:5], refs[6]
    load_state(pieces, state)
    start, stop = table[1, 2 - dy], table[1, 3 - dy]
    add_tiles(table, start, stop, 8, FIRST[2], held, state, acc)
    for half, out in enumerate(outs):
        for s in range(8):
            out[s] = acc[dy * 16 + half * 8 + s].astype(BF)


def tile_sums(table, tiles, held, first, second, late):
    acc_type = jax.ShapeDtypeStruct((N_SLOT + 1, B, B), F32)
    n_tiles = tiles.shape[0]
    blocks = [pltpu.VMEM((stop - start, B, B), BF) for start, stop in zip(FIRST, FIRST[1:])]
    if held is None:
        acc, held = pl.pallas_call(
            fetch_kernel,
            out_shape=(acc_type, jax.ShapeDtypeStruct(tiles.shape, BF)),
            in_specs=[SMEM, HBM] + [VMEM] * len(first),
            out_specs=(VMEM, VMEM),
            scratch_shapes=[blocks[0], pltpu.SemaphoreType.DMA((n_tiles // GROUP,))],
            compiler_params=PARAMS,
            cost_estimate=cost(100, 0),
            name="fetch_tiles",
        )(table, tiles, *first)
    else:
        acc = pl.pallas_call(
            first_kernel,
            out_shape=acc_type,
            in_specs=[SMEM] + [VMEM] * (1 + len(first)),
            out_specs=VMEM,
            scratch_shapes=[blocks[0]],
            compiler_params=PARAMS,
            cost_estimate=cost(50, 0),
            name="first_tiles",
        )(table, held, *first)
    acc = pl.pallas_call(
        second_kernel,
        out_shape=acc_type,
        in_specs=[SMEM] + [VMEM] * (2 + len(second)),
        out_specs=VMEM,
        scratch_shapes=[blocks[1]],
        input_output_aliases={2: 0},
        compiler_params=PARAMS,
        cost_estimate=cost(50, 0),
        name="second_tiles",
    )(table, held, acc, *second)
    out = jax.ShapeDtypeStruct((8, B, B), BF)
    sums = []
    for dy in (1, 0):
        keep, send, acc = pl.pallas_call(
            functools.partial(late_kernel, dy),
            out_shape=(out, out, acc_type),
            in_specs=[SMEM] + [VMEM] * (2 + len(late)),
            out_specs=(VMEM,) * 3,
            scratch_shapes=[blocks[2]],
            input_output_aliases={2: 2},
            compiler_params=PARAMS,
            cost_estimate=cost(160, 0),
            name=f"late_tiles_{dy}",
        )(table, held, acc, *late)
        sums = [keep, send] + sums
    return sums, held


def gather(state):
    far = lax.ppermute(state, "row", X_FAR)
    near = lax.ppermute(state, "row", Y_HI)
    up = lax.ppermute(state, "row", X_UP)
    down = lax.ppermute(state, "row", X_DOWN)
    near_up = lax.ppermute(near, "row", X_UP)
    near_down = lax.ppermute(near, "row", X_DOWN)
    near_far = lax.ppermute(far, "row", Y_HI)
    return (state, near, far), (up, down), (near_up, near_down, near_far)


def add(*terms):
    total = terms[0].astype(F32)
    for term in terms[1:]:
        total = total + term.astype(F32)
    return total


def add_kernel(*refs):
    terms, out = refs[:-1], refs[-1]
    for k in range(2):
        out[k] = add(*(term[k] for term in terms)).astype(out.dtype)


def add_blocks(dtype, claim, *terms):
    return pl.pallas_call(
        add_kernel,
        out_shape=jax.ShapeDtypeStruct((2, B, B), dtype),
        in_specs=[VMEM] * len(terms),
        out_specs=VMEM,
        compiler_params=PARAMS,
        cost_estimate=cost(claim, 0),
        name="add_blocks",
    )(*terms)


def col_sum(keep_0, send_0, keep_1, send_1):
    other_1 = lax.ppermute(send_1, "col", CORE)
    other_0 = lax.ppermute(send_0, "col", CORE)
    far_1 = add(keep_1[4:6], other_1[4:6]).astype(BF)
    across_far = lax.ppermute(far_1, "col", Y_LO)
    low_1 = lax.ppermute(add(keep_1[2:4], other_1[2:4]).astype(BF), "col", Z_UP)
    high_1 = lax.ppermute(add(keep_1[6:8], other_1[6:8]).astype(BF), "col", Z_DOWN)
    low_0 = lax.ppermute(add(keep_0[2:4], other_0[2:4]).astype(BF), "col", Z_UP)
    high_0 = lax.ppermute(add(keep_0[6:8], other_0[6:8]).astype(BF), "col", Z_DOWN)
    far_0 = add(keep_0[4:6], other_0[4:6])
    far = lax.ppermute(add_blocks(BF, 0, far_0, across_far), "col", Z_FAR)
    out = add_blocks(BF, 0, keep_1, other_1, low_1, high_1)
    across = lax.ppermute(out, "col", Y_LO)
    near = add_blocks(F32, 300, keep_0, other_0, low_0, high_0)
    return near, far, across


def update_kernel(flags, weight, inject, state, *refs):
    terms, (new, residual) = refs[:3], refs[3:]
    for k in range(2):
        total = add(*(term[k] for term in terms))
        pre = jnp.dot(total.astype(BF), weight[...], preferred_element_type=F32)
        rows = pl.ds(k * B, B)
        old = state[rows]
        updated = jnp.tanh(pre + inject[rows].astype(F32)).astype(BF)
        updated = jnp.where(flags[k] == 1, old, updated)
        new[rows] = updated
        change = updated.astype(F32) - old.astype(F32)
        residual[k] = jnp.sum(change * change)


def update(flags, weight, inject, state, terms):
    return pl.pallas_call(
        update_kernel,
        out_shape=(
            jax.ShapeDtypeStruct(state.shape, BF),
            jax.ShapeDtypeStruct((2,), F32),
        ),
        in_specs=[SMEM] + [VMEM] * 6,
        out_specs=(VMEM, SMEM),
        compiler_params=PARAMS,
        cost_estimate=cost(2, 0),
        name="update",
    )(flags, weight, inject, state, *terms)


def per_device(features, inject, weight, tiles, tile_rows, tile_cols, tile_count, flags):
    tile_set = pltpu.with_memory_space_constraint(tiles[0, 0], pltpu.HBM)
    in_hbm = [
        pltpu.with_memory_space_constraint(value, pltpu.HBM)
        for value in (tile_rows[0], tile_cols[0], features)
    ]
    table, state = prepare(in_hbm[0], in_hbm[1], tile_count[0], in_hbm[2])
    held = None
    for step in range(ITERS):
        sums, held = tile_sums(table, tile_set, held, *gather(state))
        state, residual = update(flags, weight, inject, state, col_sum(*sums))
    return state, residual


def solution(mesh):
    in_specs = (
        P(("row", "col"), None),
        P(("row", "col"), None),
        P(),
        P("row", "col", None, None, None),
        P("row", "col", None),
        P("row", "col", None),
        P("row", "col"),
        P(("row", "col")),
    )
    out_specs = (P(("row", "col"), None), P(("row", "col")))
    return jax.shard_map(
        per_device, mesh=mesh, in_specs=in_specs, out_specs=out_specs, check_vma=False
    )
```

time: 125 us -> 108 us (0.86); the launches traced: 125 us -> 106 us
  starting transfers between devices: 55.9 us -> 42.8 us
  other arithmetic: 4.49 us -> 0.78 us
  waiting for transfers between devices: 45.1 us -> 41.9 us
    ppermute x24 -> x18, waiting for transfers between devices: 34.2 us -> 21.6 us  [the longest x2 6.05 us: col_sum(): far = lax.ppermute(add_blocks(BF, 0, far_0, across_far), 'col', Z_FAR)]
    ppermute x24 -> x18, starting transfers between devices: 36.1 us -> 24.5 us  [the longest x2 6.49 us: col_sum(): far = lax.ppermute(add_blocks(BF, 0, far_0, across_far), 'col', Z_FAR)]
    ppermute x2, waiting for transfers between devices: 0.01 us -> 4.56 us  [gather(): near_down = lax.ppermute(near, 'row', X_DOWN)]
    ppermute x2, starting transfers between devices: 5.61 us -> 1.09 us  [gather(): near_up = lax.ppermute(near, 'row', X_UP)]
    ppermute x2, waiting for transfers between devices: 0.01 us -> 3.38 us  [gather(): near_up = lax.ppermute(near, 'row', X_UP)]
    ppermute x2, starting transfers between devices: 3.33 us -> 6.4 us  [gather(): near = lax.ppermute(state, 'row', Y_HI)]
    ppermute x2, waiting for transfers between devices: 2.68 us -> 5.27 us  [gather(): near = lax.ppermute(state, 'row', Y_HI)]
    pallas_call x4 -> x14, Pallas kernels: 9.73 us -> 12 us  [the longest x4 6.2 us: tile_sums(): pl.pallas_call(functools.partial(late_kernel, dy), out_shape=(out, out, a...]
  transfers between devices with their start and end apart: 38 -> 32, of which waited for: 15 -> 23; matrix products, arithmetic and copies ran while one was open for 4% -> 1% of each run, Pallas kernels for 7% -> 10%
where the time goes in v3:
time: 108 us; the launch traced here: 106 us
  starting transfers between devices  42.8 us (40%)
  waiting for transfers between devices  41.9 us (39%)
  Pallas kernels  18.6 us (17%)
  between operations  1.65 us (2%)
    ppermute x2, starting transfers between devices, col_sum(): far = lax.ppermute(add_blocks(BF, 0, far_0, across_far), 'col', Z_FAR)  6.49 us
    ppermute x2, starting transfers between devices, gather(): near = lax.ppermute(state, 'row', Y_HI)  6.4 us
    pallas_call x4, Pallas kernels, tile_sums(): pl.pallas_call(functools.partial(late_kernel, dy), out_shape=(out, out, a...  6.2 us
    ppermute x2, waiting for transfers between devices, col_sum(): far = lax.ppermute(add_blocks(BF, 0, far_0, across_far), 'col', Z_FAR)  6.05 us
    ppermute x2, starting transfers between devices, col_sum(): low_1 = lax.ppermute(add(keep_1[2:4], other_1[2:4]).astype(BF), 'col', Z_UP)  5.78 us
    ppermute x2, waiting for transfers between devices, gather(): far = lax.ppermute(state, 'row', X_FAR)  5.62 us
    ppermute x2, starting transfers between devices, col_sum(): lax.ppermute(add(keep_0[6:8], other_0[6:8]).astype(BF), 'col', Z_DOWN)  5.54 us
    ppermute x2, waiting for transfers between devices, gather(): near = lax.ppermute(state, 'row', Y_HI)  5.27 us
  transfers between devices with their start and end apart: 32, of which 23 were waited for; matrix products, arithmetic and copies ran while one was open for 1% of the time, Pallas kernels for 10%

profile of v3, /device:TPU:6, one launch (start us, length us, event | category | flops | bytes accessed | tf_op | source)
XLA Modules:
  0.0 105.7 jit_solution(12498469826632953808)
XLA Ops:
  2.3 3.3 %collective-permute-start = (bf16[512,256]{1,0:T(8,128)(2,1)S(1)}, bf16[512,256]{1,0:T(8,128)(2,1)S(1)}, u32[]{:S(2)}, u32[]{:S(2)}) collective-permute-start(bf16[512,256]{1,0:T(8,128)(2,1)S(1)} %get-tuple-element.17.refs_0_.state), channel_id=1, source_target_pairs={{0,16},{16,0},{32,48},{48,32},{64,80},{80,64},{96,112},{112,96},{1... | collective-permute-start | bytes 786440 | tf_op jit(solution)/shard_map/ppermute | solution.py:252
  7.0 2.1 %collective-permute-start.2 = (bf16[512,256]{1,0:T(8,128)(2,1)S(1)}, bf16[512,256]{1,0:T(8,128)(2,1)S(1)}, u32[]{:S(2)}, u32[]{:S(2)}) collective-permute-start(bf16[512,256]{1,0:T(8,128)(2,1)S(1)} %get-tuple-element.17.refs_0_.state), channel_id=1, source_target_pairs={{0,32},{16,48},{32,64},{48,80},{64,96},{80,112},{96,0},{112,16},{1... | collective-permute-start | bytes 786440 | tf_op jit(solution)/shard_map/ppermute | solution.py:253
  9.1 2.8 %collective-permute-done.refs_1_ = bf16[512,256]{1,0:T(8,128)(2,1)S(1)} collective-permute-done((bf16[512,256]{1,0:T(8,128)(2,1)S(1)}, bf16[512,256]{1,0:T(8,128)(2,1)S(1)}, u32[]{:S(2)}, u32[]{:S(2)}) %collective-permute-start) | collective-permute-done | bytes 262176 | tf_op jit(solution)/shard_map/ppermute | solution.py:252
  13.9 2.4 %collective-permute-done.1.refs_2_ = bf16[512,256]{1,0:T(8,128)(2,1)S(1)} collective-permute-done((bf16[512,256]{1,0:T(8,128)(2,1)S(1)}, bf16[512,256]{1,0:T(8,128)(2,1)S(1)}, u32[]{:S(2)}, u32[]{:S(2)}) %collective-permute-start.1) | collective-permute-done | bytes 262176 | tf_op jit(solution)/shard_map/ppermute | solution.py:251
  17.1 3.5 %fetch_tiles.1 = (f32[33,256,256]{2,1,0:T(8,128)S(1)}, bf16[128,256,256]{2,1,0:T(8,128)(2,1)S(1)}) custom-call(s32[2,128]{1,0:T(2,128)S(1)} %get-tuple-element.18.table, bf16[128,256,256]{2,1,0:T(8,128)(2,1)} %bitcast.5, bf16[512,256]{1,0:T(8,128)(2,1)S(1)} %get-tuple-element.17.refs_0_.state, bf16[512,256]{1,0:T(8,128)(2,1)S(1)} %collective-permute-done.refs_1_, ...), custom_call_target="tpu_custom_call" | custom-call | flops 3355443200 | tf_op jit(solution)/shard_map/fetch_tiles/pallas_call | solution.py:200
  21.8 2.1 %collective-permute-done.4.refs_0_ = bf16[512,256]{1,0:T(8,128)(2,1)S(1)} collective-permute-done((bf16[512,256]{1,0:T(8,128)(2,1)S(1)}, bf16[512,256]{1,0:T(8,128)(2,1)S(1)}, u32[]{:S(2)}, u32[]{:S(2)}) %collective-permute-start.4) | collective-permute-done | bytes 262176 | tf_op jit(solution)/shard_map/ppermute | solution.py:255
  23.9 2.2 %collective-permute-done.5.refs_1_ = bf16[512,256]{1,0:T(8,128)(2,1)S(1)} collective-permute-done((bf16[512,256]{1,0:T(8,128)(2,1)S(1)}, bf16[512,256]{1,0:T(8,128)(2,1)S(1)}, u32[]{:S(2)}, u32[]{:S(2)}) %collective-permute-start.5) | collective-permute-done | bytes 262176 | tf_op jit(solution)/shard_map/ppermute | solution.py:256
  30.8 4.1 %collective-permute-start.13 = (bf16[2,256,256]{2,1,0:T(8,128)(2,1)S(1)}, bf16[2,256,256]{2,1,0:T(8,128)(2,1)S(1)}, u32[]{:S(2)}, u32[]{:S(2)}) collective-permute-start(bf16[2,256,256]{2,1,0:T(8,128)(2,1)S(1)} %get-tuple-element.39), channel_id=1, source_target_pairs={{0,2},{1,3},{2,4},{3,5},{4,6},{5,7},{6,0},{7,1},{8,10},{9,11},{10,... | collective-permute-start | bytes 786440 | tf_op jit(solution)/shard_map/ppermute | solution.py:291
  37.6 2.3 %collective-permute-start.9 = (bf16[2,256,256]{2,1,0:T(8,128)(2,1)S(1)}, bf16[2,256,256]{2,1,0:T(8,128)(2,1)S(1)}, u32[]{:S(2)}, u32[]{:S(2)}) collective-permute-start(bf16[2,256,256]{2,1,0:T(8,128)(2,1)S(1)} %get-tuple-element.42), channel_id=1, source_target_pairs={{0,6},{1,7},{2,0},{3,1},{4,2},{5,3},{6,4},{7,5},{8,14},{9,15},{10,... | collective-permute-start | bytes 786440 | tf_op jit(solution)/shard_map/ppermute | solution.py:294
  39.9 2.1 %collective-permute-done.13.refs_2_ = bf16[2,256,256]{2,1,0:T(8,128)(2,1)S(1)} collective-permute-done((bf16[2,256,256]{2,1,0:T(8,128)(2,1)S(1)}, bf16[2,256,256]{2,1,0:T(8,128)(2,1)S(1)}, u32[]{:S(2)}, u32[]{:S(2)}) %collective-permute-start.13) | collective-permute-done | bytes 262176 | tf_op jit(solution)/shard_map/ppermute | solution.py:291
  42.0 2.1 %collective-permute-done.14.refs_3_ = bf16[2,256,256]{2,1,0:T(8,128)(2,1)S(1)} collective-permute-done((bf16[2,256,256]{2,1,0:T(8,128)(2,1)S(1)}, bf16[2,256,256]{2,1,0:T(8,128)(2,1)S(1)}, u32[]{:S(2)}, u32[]{:S(2)}) %collective-permute-start.14) | collective-permute-done | bytes 262176 | tf_op jit(solution)/shard_map/ppermute | solution.py:292
  44.4 3.0 %collective-permute-start.12 = (bf16[2,256,256]{2,1,0:T(8,128)(2,1)S(1)}, bf16[2,256,256]{2,1,0:T(8,128)(2,1)S(1)}, u32[]{:S(2)}, u32[]{:S(2)}) collective-permute-start(bf16[2,256,256]{2,1,0:T(8,128)(2,1)S(1)} %add_blocks.7), channel_id=1, source_target_pairs={{0,4},{1,5},{2,6},{3,7},{4,0},{5,1},{6,2},{7,3},{8,12},{9,13},{10,... | collective-permute-start | bytes 786440 | tf_op jit(solution)/shard_map/ppermute | solution.py:296
  47.4 2.3 %collective-permute-done.9.refs_3_ = bf16[2,256,256]{2,1,0:T(8,128)(2,1)S(1)} collective-permute-done((bf16[2,256,256]{2,1,0:T(8,128)(2,1)S(1)}, bf16[2,256,256]{2,1,0:T(8,128)(2,1)S(1)}, u32[]{:S(2)}, u32[]{:S(2)}) %collective-permute-start.9) | collective-permute-done | bytes 262176 | tf_op jit(solution)/shard_map/ppermute | solution.py:294
  51.2 2.8 %collective-permute-done.12.refs_1_ = bf16[2,256,256]{2,1,0:T(8,128)(2,1)S(1)} collective-permute-done((bf16[2,256,256]{2,1,0:T(8,128)(2,1)S(1)}, bf16[2,256,256]{2,1,0:T(8,128)(2,1)S(1)}, u32[]{:S(2)}, u32[]{:S(2)}) %collective-permute-start.12) | collective-permute-done | bytes 262176 | tf_op jit(solution)/shard_map/ppermute | solution.py:296
  55.5 3.1 %collective-permute-start.16 = (bf16[512,256]{1,0:T(8,128)(2,1)S(1)}, bf16[512,256]{1,0:T(8,128)(2,1)S(1)}, u32[]{:S(2)}, u32[]{:S(2)}) collective-permute-start(bf16[512,256]{1,0:T(8,128)(2,1)S(1)} %get-tuple-element.26.refs_0_.state), channel_id=1, source_target_pairs={{0,16},{16,0},{32,48},{48,32},{64,80},{80,64},{96,112},{112,96},{1... | collective-permute-start | bytes 786440 | tf_op jit(solution)/shard_map/ppermute | solution.py:252
  61.6 2.4 %collective-permute-done.16.refs_1_ = bf16[512,256]{1,0:T(8,128)(2,1)S(1)} collective-permute-done((bf16[512,256]{1,0:T(8,128)(2,1)S(1)}, bf16[512,256]{1,0:T(8,128)(2,1)S(1)}, u32[]{:S(2)}, u32[]{:S(2)}) %collective-permute-start.16) | collective-permute-done | bytes 262176 | tf_op jit(solution)/shard_map/ppermute | solution.py:252
  66.1 3.3 %collective-permute-done.17.refs_2_ = bf16[512,256]{1,0:T(8,128)(2,1)S(1)} collective-permute-done((bf16[512,256]{1,0:T(8,128)(2,1)S(1)}, bf16[512,256]{1,0:T(8,128)(2,1)S(1)}, u32[]{:S(2)}, u32[]{:S(2)}) %collective-permute-start.17) | collective-permute-done | bytes 262176 | tf_op jit(solution)/shard_map/ppermute | solution.py:251
  69.8 2.0 %first_tiles.1.acc = f32[33,256,256]{2,1,0:T(8,128)S(1)} custom-call(s32[2,128]{1,0:T(2,128)S(1)} %get-tuple-element.18.table, bf16[128,256,256]{2,1,0:T(8,128)(2,1)S(1)} %get-tuple-element.19.held, bf16[512,256]{1,0:T(8,128)(2,1)S(1)} %get-tuple-element.26.refs_0_.state, bf16[512,256]{1,0:T(8,128)(2,1)S(1)} %collective-permute-done.16.refs_1_, ...), custom_call_target="tpu_custom_call" | custom-call | flops 1677721600 | tf_op jit(solution)/shard_map/first_tiles/pallas_call | solution.py:211
  75.7 2.4 %collective-permute-done.21.refs_1_ = bf16[512,256]{1,0:T(8,128)(2,1)S(1)} collective-permute-done((bf16[512,256]{1,0:T(8,128)(2,1)S(1)}, bf16[512,256]{1,0:T(8,128)(2,1)S(1)}, u32[]{:S(2)}, u32[]{:S(2)}) %collective-permute-start.21) | collective-permute-done | bytes 262176 | tf_op jit(solution)/shard_map/ppermute | solution.py:256
  78.1 1.8 %late_tiles_1.3 = (bf16[8,256,256]{2,1,0:T(8,128)(2,1)S(1)}, bf16[8,256,256]{2,1,0:T(8,128)(2,1)S(1)}, f32[33,256,256]{2,1,0:T(8,128)S(1)}) custom-call(s32[2,128]{1,0:T(2,128)S(1)} %get-tuple-element.18.table, bf16[128,256,256]{2,1,0:T(8,128)(2,1)S(1)} %get-tuple-element.19.held, ...), custom_call_target="tpu_custom_call", output_to_operand_aliasing={{2}: (2, {})} | custom-call | flops 5368709120 | tf_op jit(solution)/shard_map/late_tiles_1/pallas_call | solution.py:235
  87.1 3.2 %collective-permute-start.25 = (bf16[2,256,256]{2,1,0:T(8,128)(2,1)S(1)}, bf16[2,256,256]{2,1,0:T(8,128)(2,1)S(1)}, u32[]{:S(2)}, u32[]{:S(2)}) collective-permute-start(bf16[2,256,256]{2,1,0:T(8,128)(2,1)S(1)} %get-tuple-element.36), channel_id=1, source_target_pairs={{0,6},{1,7},{2,0},{3,1},{4,2},{5,3},{6,4},{7,5},{8,14},{9,15},{10,... | collective-permute-start | bytes 786440 | tf_op jit(solution)/shard_map/ppermute | solution.py:294
  90.3 3.0 %collective-permute-done.29.refs_2_ = bf16[2,256,256]{2,1,0:T(8,128)(2,1)S(1)} collective-permute-done((bf16[2,256,256]{2,1,0:T(8,128)(2,1)S(1)}, bf16[2,256,256]{2,1,0:T(8,128)(2,1)S(1)}, u32[]{:S(2)}, u32[]{:S(2)}) %collective-permute-start.29) | collective-permute-done | bytes 262176 | tf_op jit(solution)/shard_map/ppermute | solution.py:291
  94.2 3.5 %collective-permute-start.28 = (bf16[2,256,256]{2,1,0:T(8,128)(2,1)S(1)}, bf16[2,256,256]{2,1,0:T(8,128)(2,1)S(1)}, u32[]{:S(2)}, u32[]{:S(2)}) collective-permute-start(bf16[2,256,256]{2,1,0:T(8,128)(2,1)S(1)} %add_blocks.10), channel_id=1, source_target_pairs={{0,4},{1,5},{2,6},{3,7},{4,0},{5,1},{6,2},{7,3},{8,12},{9,13},{10,... | collective-permute-start | bytes 786440 | tf_op jit(solution)/shard_map/ppermute | solution.py:296
  100.7 3.3 %collective-permute-done.28.refs_1_ = bf16[2,256,256]{2,1,0:T(8,128)(2,1)S(1)} collective-permute-done((bf16[2,256,256]{2,1,0:T(8,128)(2,1)S(1)}, bf16[2,256,256]{2,1,0:T(8,128)(2,1)S(1)}, u32[]{:S(2)}, u32[]{:S(2)}) %collective-permute-start.28) | collective-permute-done | bytes 262176 | tf_op jit(solution)/shard_map/ppermute | solution.py:296
  (67 shorter events, 39.0 us)
Async XLA Ops:
  2.3 9.6 %collective-permute-start = (bf16[512,256]{1,0:T(8,128)(2,1)S(1)}, bf16[512,256]{1,0:T(8,128)(2,1)S(1)}, u32[]{:S(2)}, u32[]{:S(2)}) collective-permute-start(bf16[512,256]{1,0:T(8,128)(2,1)S(1)} %get-tuple-element.17.refs_0_.state), channel_id=1, source_target_pairs={{0,16},{16,0},{32,48},{48,32},{64,80},{80,64},{96,112},{112,96},{1... | collective-permute-start | bytes 786440 | tf_op jit(solution)/shard_map/ppermute | solution.py:252
  5.6 10.7 %collective-permute-start.1 = (bf16[512,256]{1,0:T(8,128)(2,1)S(1)}, bf16[512,256]{1,0:T(8,128)(2,1)S(1)}, u32[]{:S(2)}, u32[]{:S(2)}) collective-permute-start(bf16[512,256]{1,0:T(8,128)(2,1)S(1)} %get-tuple-element.17.refs_0_.state), channel_id=1, source_target_pairs={{0,64},{16,80},{32,96},{48,112},{64,0},{80,16},{96,32},{112,48},{1... | collective-permute-start | bytes 786440 | tf_op jit(solution)/shard_map/ppermute | solution.py:251
  7.0 13.7 %collective-permute-start.2 = (bf16[512,256]{1,0:T(8,128)(2,1)S(1)}, bf16[512,256]{1,0:T(8,128)(2,1)S(1)}, u32[]{:S(2)}, u32[]{:S(2)}) collective-permute-start(bf16[512,256]{1,0:T(8,128)(2,1)S(1)} %get-tuple-element.17.refs_0_.state), channel_id=1, source_target_pairs={{0,32},{16,48},{32,64},{48,80},{64,96},{80,112},{96,0},{112,16},{1... | collective-permute-start | bytes 786440 | tf_op jit(solution)/shard_map/ppermute | solution.py:253
  9.1 11.6 %collective-permute-start.3 = (bf16[512,256]{1,0:T(8,128)(2,1)S(1)}, bf16[512,256]{1,0:T(8,128)(2,1)S(1)}, u32[]{:S(2)}, u32[]{:S(2)}) collective-permute-start(bf16[512,256]{1,0:T(8,128)(2,1)S(1)} %get-tuple-element.17.refs_0_.state), channel_id=1, source_target_pairs={{0,96},{16,112},{32,0},{48,16},{64,32},{80,48},{96,64},{112,80},{1... | collective-permute-start | bytes 786440 | tf_op jit(solution)/shard_map/ppermute | solution.py:254
  11.9 12.0 %collective-permute-start.4 = (bf16[512,256]{1,0:T(8,128)(2,1)S(1)}, bf16[512,256]{1,0:T(8,128)(2,1)S(1)}, u32[]{:S(2)}, u32[]{:S(2)}) collective-permute-start(bf16[512,256]{1,0:T(8,128)(2,1)S(1)} %collective-permute-done.refs_1_), channel_id=1, source_target_pairs={{0,32},{16,48},{32,64},{48,80},{64,96},{80,112},{96,0},{112,16},{1... | collective-permute-start | bytes 786440 | tf_op jit(solution)/shard_map/ppermute | solution.py:255
  12.4 13.7 %collective-permute-start.5 = (bf16[512,256]{1,0:T(8,128)(2,1)S(1)}, bf16[512,256]{1,0:T(8,128)(2,1)S(1)}, u32[]{:S(2)}, u32[]{:S(2)}) collective-permute-start(bf16[512,256]{1,0:T(8,128)(2,1)S(1)} %collective-permute-done.refs_1_), channel_id=1, source_target_pairs={{0,96},{16,112},{32,0},{48,16},{64,32},{80,48},{96,64},{112,80},{1... | collective-permute-start | bytes 786440 | tf_op jit(solution)/shard_map/ppermute | solution.py:256
  16.3 9.8 %collective-permute-start.6 = (bf16[512,256]{1,0:T(8,128)(2,1)S(1)}, bf16[512,256]{1,0:T(8,128)(2,1)S(1)}, u32[]{:S(2)}, u32[]{:S(2)}) collective-permute-start(bf16[512,256]{1,0:T(8,128)(2,1)S(1)} %collective-permute-done.1.refs_2_), channel_id=1, source_target_pairs={{0,16},{16,0},{32,48},{48,32},{64,80},{80,64},{96,112},{112,96},{1... | collective-permute-start | bytes 786440 | tf_op jit(solution)/shard_map/ppermute | solution.py:257
  30.8 11.2 %collective-permute-start.13 = (bf16[2,256,256]{2,1,0:T(8,128)(2,1)S(1)}, bf16[2,256,256]{2,1,0:T(8,128)(2,1)S(1)}, u32[]{:S(2)}, u32[]{:S(2)}) collective-permute-start(bf16[2,256,256]{2,1,0:T(8,128)(2,1)S(1)} %get-tuple-element.39), channel_id=1, source_target_pairs={{0,2},{1,3},{2,4},{3,5},{4,6},{5,7},{6,0},{7,1},{8,10},{9,11},{10,... | collective-permute-start | bytes 786440 | tf_op jit(solution)/shard_map/ppermute | solution.py:291
  35.0 9.1 %collective-permute-start.14 = (bf16[2,256,256]{2,1,0:T(8,128)(2,1)S(1)}, bf16[2,256,256]{2,1,0:T(8,128)(2,1)S(1)}, u32[]{:S(2)}, u32[]{:S(2)}) collective-permute-start(bf16[2,256,256]{2,1,0:T(8,128)(2,1)S(1)} %get-tuple-element.38), channel_id=1, source_target_pairs={{0,6},{1,7},{2,0},{3,1},{4,2},{5,3},{6,4},{7,5},{8,14},{9,15},{10,... | collective-permute-start | bytes 786440 | tf_op jit(solution)/shard_map/ppermute | solution.py:292
  35.0 9.3 %collective-permute-start.11 = (bf16[2,256,256]{2,1,0:T(8,128)(2,1)S(1)}, bf16[2,256,256]{2,1,0:T(8,128)(2,1)S(1)}, u32[]{:S(2)}, u32[]{:S(2)}) collective-permute-start(bf16[2,256,256]{2,1,0:T(8,128)(2,1)S(1)} %get-tuple-element.40), channel_id=1, source_target_pairs={{0,8},{1,9},{2,10},{3,11},{4,12},{5,13},{6,14},{7,15},{8,0},{9,1},... | collective-permute-start | bytes 786440 | tf_op jit(solution)/shard_map/ppermute | solution.py:290
  36.6 10.8 %collective-permute-start.8 = (bf16[2,256,256]{2,1,0:T(8,128)(2,1)S(1)}, bf16[2,256,256]{2,1,0:T(8,128)(2,1)S(1)}, u32[]{:S(2)}, u32[]{:S(2)}) collective-permute-start(bf16[2,256,256]{2,1,0:T(8,128)(2,1)S(1)} %get-tuple-element.43), channel_id=1, source_target_pairs={{0,2},{1,3},{2,4},{3,5},{4,6},{5,7},{6,0},{7,1},{8,10},{9,11},{10,... | collective-permute-start | bytes 786440 | tf_op jit(solution)/shard_map/ppermute | solution.py:293
  37.6 12.1 %collective-permute-start.9 = (bf16[2,256,256]{2,1,0:T(8,128)(2,1)S(1)}, bf16[2,256,256]{2,1,0:T(8,128)(2,1)S(1)}, u32[]{:S(2)}, u32[]{:S(2)}) collective-permute-start(bf16[2,256,256]{2,1,0:T(8,128)(2,1)S(1)} %get-tuple-element.42), channel_id=1, source_target_pairs={{0,6},{1,7},{2,0},{3,1},{4,2},{5,3},{6,4},{7,5},{8,14},{9,15},{10,... | collective-permute-start | bytes 786440 | tf_op jit(solution)/shard_map/ppermute | solution.py:294
  44.4 9.5 %collective-permute-start.12 = (bf16[2,256,256]{2,1,0:T(8,128)(2,1)S(1)}, bf16[2,256,256]{2,1,0:T(8,128)(2,1)S(1)}, u32[]{:S(2)}, u32[]{:S(2)}) collective-permute-start(bf16[2,256,256]{2,1,0:T(8,128)(2,1)S(1)} %add_blocks.7), channel_id=1, source_target_pairs={{0,4},{1,5},{2,6},{3,7},{4,0},{5,1},{6,2},{7,3},{8,12},{9,13},{10,... | collective-permute-start | bytes 786440 | tf_op jit(solution)/shard_map/ppermute | solution.py:296
  58.6 10.7 %collective-permute-start.17 = (bf16[512,256]{1,0:T(8,128)(2,1)S(1)}, bf16[512,256]{1,0:T(8,128)(2,1)S(1)}, u32[]{:S(2)}, u32[]{:S(2)}) collective-permute-start(bf16[512,256]{1,0:T(8,128)(2,1)S(1)} %get-tuple-element.26.refs_0_.state), channel_id=1, source_target_pairs={{0,64},{16,80},{32,96},{48,112},{64,0},{80,16},{96,32},{112,48},{1... | collective-permute-start | bytes 786440 | tf_op jit(solution)/shard_map/ppermute | solution.py:251
  59.6 13.2 %collective-permute-start.18 = (bf16[512,256]{1,0:T(8,128)(2,1)S(1)}, bf16[512,256]{1,0:T(8,128)(2,1)S(1)}, u32[]{:S(2)}, u32[]{:S(2)}) collective-permute-start(bf16[512,256]{1,0:T(8,128)(2,1)S(1)} %get-tuple-element.26.refs_0_.state), channel_id=1, source_target_pairs={{0,32},{16,48},{32,64},{48,80},{64,96},{80,112},{96,0},{112,16},{1... | collective-permute-start | bytes 786440 | tf_op jit(solution)/shard_map/ppermute | solution.py:253
  61.2 12.2 %collective-permute-start.19 = (bf16[512,256]{1,0:T(8,128)(2,1)S(1)}, bf16[512,256]{1,0:T(8,128)(2,1)S(1)}, u32[]{:S(2)}, u32[]{:S(2)}) collective-permute-start(bf16[512,256]{1,0:T(8,128)(2,1)S(1)} %get-tuple-element.26.refs_0_.state), channel_id=1, source_target_pairs={{0,96},{16,112},{32,0},{48,16},{64,32},{80,48},{96,64},{112,80},{1... | collective-permute-start | bytes 786440 | tf_op jit(solution)/shard_map/ppermute | solution.py:254
  64.1 11.6 %collective-permute-start.20 = (bf16[512,256]{1,0:T(8,128)(2,1)S(1)}, bf16[512,256]{1,0:T(8,128)(2,1)S(1)}, u32[]{:S(2)}, u32[]{:S(2)}) collective-permute-start(bf16[512,256]{1,0:T(8,128)(2,1)S(1)} %collective-permute-done.16.refs_1_), channel_id=1, source_target_pairs={{0,32},{16,48},{32,64},{48,80},{64,96},{80,112},{96,0},{112,16},{1... | collective-permute-start | bytes 786440 | tf_op jit(solution)/shard_map/ppermute | solution.py:255
  64.7 13.3 %collective-permute-start.21 = (bf16[512,256]{1,0:T(8,128)(2,1)S(1)}, bf16[512,256]{1,0:T(8,128)(2,1)S(1)}, u32[]{:S(2)}, u32[]{:S(2)}) collective-permute-start(bf16[512,256]{1,0:T(8,128)(2,1)S(1)} %collective-permute-done.16.refs_1_), channel_id=1, source_target_pairs={{0,96},{16,112},{32,0},{48,16},{64,32},{80,48},{96,64},{112,80},{1... | collective-permute-start | bytes 786440 | tf_op jit(solution)/shard_map/ppermute | solution.py:256
  69.4 8.7 %collective-permute-start.22 = (bf16[512,256]{1,0:T(8,128)(2,1)S(1)}, bf16[512,256]{1,0:T(8,128)(2,1)S(1)}, u32[]{:S(2)}, u32[]{:S(2)}) collective-permute-start(bf16[512,256]{1,0:T(8,128)(2,1)S(1)} %collective-permute-done.17.refs_2_), channel_id=1, source_target_pairs={{0,16},{16,0},{32,48},{48,32},{64,80},{80,64},{96,112},{112,96},{1... | collective-permute-start | bytes 786440 | tf_op jit(solution)/shard_map/ppermute | solution.py:257
  82.8 10.4 %collective-permute-start.29 = (bf16[2,256,256]{2,1,0:T(8,128)(2,1)S(1)}, bf16[2,256,256]{2,1,0:T(8,128)(2,1)S(1)}, u32[]{:S(2)}, u32[]{:S(2)}) collective-permute-start(bf16[2,256,256]{2,1,0:T(8,128)(2,1)S(1)} %get-tuple-element.33), channel_id=1, source_target_pairs={{0,2},{1,3},{2,4},{3,5},{4,6},{5,7},{6,0},{7,1},{8,10},{9,11},{10,... | collective-permute-start | bytes 786440 | tf_op jit(solution)/shard_map/ppermute | solution.py:291
  84.5 9.1 %collective-permute-start.30 = (bf16[2,256,256]{2,1,0:T(8,128)(2,1)S(1)}, bf16[2,256,256]{2,1,0:T(8,128)(2,1)S(1)}, u32[]{:S(2)}, u32[]{:S(2)}) collective-permute-start(bf16[2,256,256]{2,1,0:T(8,128)(2,1)S(1)} %get-tuple-element.32), channel_id=1, source_target_pairs={{0,6},{1,7},{2,0},{3,1},{4,2},{5,3},{6,4},{7,5},{8,14},{9,15},{10,... | collective-permute-start | bytes 786440 | tf_op jit(solution)/shard_map/ppermute | solution.py:292
  87.0 11.6 %collective-permute-start.24 = (bf16[2,256,256]{2,1,0:T(8,128)(2,1)S(1)}, bf16[2,256,256]{2,1,0:T(8,128)(2,1)S(1)}, u32[]{:S(2)}, u32[]{:S(2)}) collective-permute-start(bf16[2,256,256]{2,1,0:T(8,128)(2,1)S(1)} %get-tuple-element.37), channel_id=1, source_target_pairs={{0,2},{1,3},{2,4},{3,5},{4,6},{5,7},{6,0},{7,1},{8,10},{9,11},{10,... | collective-permute-start | bytes 786440 | tf_op jit(solution)/shard_map/ppermute | solution.py:293
  87.1 12.1 %collective-permute-start.25 = (bf16[2,256,256]{2,1,0:T(8,128)(2,1)S(1)}, bf16[2,256,256]{2,1,0:T(8,128)(2,1)S(1)}, u32[]{:S(2)}, u32[]{:S(2)}) collective-permute-start(bf16[2,256,256]{2,1,0:T(8,128)(2,1)S(1)} %get-tuple-element.36), channel_id=1, source_target_pairs={{0,6},{1,7},{2,0},{3,1},{4,2},{5,3},{6,4},{7,5},{8,14},{9,15},{10,... | collective-permute-start | bytes 786440 | tf_op jit(solution)/shard_map/ppermute | solution.py:294
  94.2 9.8 %collective-permute-start.28 = (bf16[2,256,256]{2,1,0:T(8,128)(2,1)S(1)}, bf16[2,256,256]{2,1,0:T(8,128)(2,1)S(1)}, u32[]{:S(2)}, u32[]{:S(2)}) collective-permute-start(bf16[2,256,256]{2,1,0:T(8,128)(2,1)S(1)} %add_blocks.10), channel_id=1, source_target_pairs={{0,4},{1,5},{2,6},{3,7},{4,0},{5,1},{6,2},{7,3},{8,12},{9,13},{10,... | collective-permute-start | bytes 786440 | tf_op jit(solution)/shard_map/ppermute | solution.py:296
  (11 other events, 77.2 us)
